TPU v7x, 256 devices: a whole 4x4x8 slice. The times are simulated.
256 devices in a mesh: seq: 16 (over z, core), expert: 16 (over y, x).
Axes of the slice: x: 4, y: 4, z: 8, core: 2. Of those that a mesh axis runs over, the one named last changes fastest.
Arguments:
- hidden_in: bfloat16 [2048, 2, 4096], P(('seq', 'expert')), may hold values from -6 to 6
- mamba_x: bfloat16 [2048, 2, 4096], P('seq', None, 'expert'), may hold values from -6 to 6
- mamba_z: bfloat16 [2048, 2, 4096], P('seq', None, 'expert'), may hold values from -6 to 6
- x_proj: bfloat16 [4096, 288], P('expert'), may hold values from -0.01171875 to 0.01171875
- dt_weight: bfloat16 [256, 4096], P(None, 'expert'), may hold values from -3 to 3
- dt_bias: float32 [4096], P('expert'), may hold values from -3 to -1
- state_rates: float32 [4096, 16], P('expert'), may hold values from 0 to 1
- skip_gain: float32 [4096], P('expert'), may hold values from 0.5 to 1.5
- out_weight: bfloat16 [4096, 4096], P('expert', 'seq'), may hold values from -0.09375 to 0.09375
- norm_gain: float32 [4096], replicated, may hold values from 0.5 to 1.5
- router_weight: bfloat16 [4096, 16], replicated, may hold values from -0.09375 to 0.09375
- expert_ids: int32 [2048, 2, 2], P(('seq', 'expert')), may hold values from 0 to 15, all different within a row; in each aligned block of 16 rows (0 to 15, 16 to 31, ..., all dimensions but the last counted through in order) at most 5 rows name the same one
- w_gate: bfloat16 [16, 4096, 7168], P('expert', None, 'seq'), may hold values from -0.09375 to 0.09375
- w_up: bfloat16 [16, 4096, 7168], P('expert', None, 'seq'), may hold values from -0.09375 to 0.09375
- w_down: bfloat16 [16, 4096, 7168], P('expert', None, 'seq'), may hold values from -0.0625 to 0.0625
Outputs:
- layer_out: bfloat16 [2048, 2, 4096], P(('seq', 'expert'))
Inputs may be any that keep to these rules, and one draw needn't show every extreme that they name: `expert_ids`: each row names 2 different experts. Taking positions and documents together in position-major order, within each aligned block of 16 rows (the rows of one device) no expert is named by more than 5 rows, a bound that some block reaches.
All inputs are finite; a program needn't handle non-finite values.
Results may differ from a plain program's by a relative error of at most 0.009.
Values may be sent and summed in bfloat16 or wider, within the bound.
A program may use at most 128 MiB of HBM per device.

v0:
```python
import jax
import jax.numpy as jnp
from jax import lax
from jax.sharding import PartitionSpec as P

EPS = 1e-05


def passed_along(block, axis, distance):
    devices = range(lax.axis_size(axis))
    route = [(i - distance, i) for i in devices if i - distance in devices]
    return lax.ppermute(block, axis, route)


def mixer_steps(step_sizes, drive, b_terms, c_terms, rates):
    unroll_count = 16
    blocks = step_sizes.shape[0] // unroll_count
    start_state = jnp.zeros((step_sizes.shape[1], step_sizes.shape[2], rates.shape[1]), jnp.float32)

    def grouped(values):
        return values.reshape((blocks, unroll_count) + values.shape[1:])

    def advance_block(state_now, inputs):
        size_block, drive_block, b_block, c_block = inputs
        readings = []
        for offset in range(unroll_count):
            decays = jnp.exp(-size_block[offset][:, :, None] * rates[None])
            state_now = (
                decays * state_now
                + (size_block[offset] * drive_block[offset])[:, :, None]
                * b_block[offset][:, None, :]
            )
            readings.append(jnp.sum(state_now * c_block[offset][:, None, :], axis=-1))
        return (state_now, jnp.stack(readings))

    final_state, readout = lax.scan(
        advance_block,
        start_state,
        (grouped(step_sizes), grouped(drive), grouped(b_terms), grouped(c_terms)),
    )
    return (final_state, readout.reshape(step_sizes.shape))


def slice_output(rows, gate_part, up_part, down_part):
    hidden = (
        jax.nn.silu(jnp.dot(rows, gate_part, preferred_element_type=jnp.float32))
        * jnp.dot(rows, up_part, preferred_element_type=jnp.float32)
    ).astype(jnp.bfloat16)
    product = lax.dot_general(
        hidden, down_part, (((1,), (1,)), ((), ())), preferred_element_type=jnp.float32
    )
    return lax.optimization_barrier(product.astype(jnp.bfloat16))


def body(
    hidden_in,
    mamba_x,
    mamba_z,
    x_proj,
    dt_weight,
    dt_bias,
    state_rates,
    skip_gain,
    out_weight,
    norm_gain,
    router_weight,
    expert_ids,
    w_gate,
    w_up,
    w_down,
):
    slice_len, docs, channels = mamba_x.shape
    rank_width = dt_weight.shape[0]
    state_width = state_rates.shape[1]
    flat_x = mamba_x.reshape(slice_len * docs, channels)
    proj = lax.psum(jnp.dot(flat_x, x_proj, preferred_element_type=jnp.float32), "expert")
    dt_low = proj[:, :rank_width].astype(jnp.bfloat16)
    step_sizes = jax.nn.softplus(
        jnp.dot(dt_low, dt_weight, preferred_element_type=jnp.float32) + dt_bias
    )
    step_sizes = step_sizes.reshape(slice_len, docs, channels)
    b_terms = proj[:, rank_width : rank_width + state_width].reshape(slice_len, docs, state_width)
    c_terms = proj[:, rank_width + state_width :].reshape(slice_len, docs, state_width)
    drive = mamba_x.astype(jnp.float32)
    zero_state = jnp.zeros((docs, channels, state_width), jnp.float32)
    local_end, local_readout = mixer_steps(step_sizes, drive, b_terms, c_terms, state_rates)
    running_sizes = jnp.cumsum(step_sizes, axis=0)
    through = jnp.exp(-running_sizes[-1][:, :, None] * state_rates[None])

    def relay_step(turn, incoming_now):
        outgoing = through * incoming_now + local_end
        return passed_along(outgoing, "seq", 1)

    incoming = lax.fori_loop(0, lax.axis_size("seq") - 1, relay_step, zero_state)
    carried_decay = jnp.exp(-running_sizes[:, :, :, None] * state_rates[None, None])
    readout = local_readout + jnp.sum(
        carried_decay * incoming[None] * c_terms[:, :, None, :], axis=-1
    )
    gated = ((readout + skip_gain * drive) * jax.nn.silu(mamba_z.astype(jnp.float32))).astype(
        jnp.bfloat16
    )
    full_out = lax.all_gather(out_weight, "seq", axis=1, tiled=True)
    model_width = full_out.shape[1]
    own_rows = slice_len // lax.axis_size("expert")
    picked_rows = lax.slice_in_dim(gated, 0, own_rows * lax.axis_size("expert"), axis=0)
    product = jnp.dot(
        picked_rows.reshape(own_rows * lax.axis_size("expert") * docs, channels),
        full_out,
        preferred_element_type=jnp.float32,
    )
    mixer = lax.psum_scatter(
        product.reshape(own_rows * lax.axis_size("expert"), docs, model_width),
        "expert",
        scatter_dimension=0,
        tiled=True,
    )
    token_rows = hidden_in.shape[0] * docs
    mixed = (
        hidden_in.reshape(token_rows, model_width).astype(jnp.float32)
        + mixer.reshape(token_rows, model_width)
    ).astype(jnp.bfloat16)
    wide = lax.optimization_barrier(mixed).astype(jnp.float32)
    normed = (
        wide * lax.rsqrt(jnp.mean(wide * wide, axis=-1, keepdims=True) + EPS) * norm_gain
    ).astype(jnp.bfloat16)
    logits = jnp.dot(normed, router_weight, preferred_element_type=jnp.float32)
    experts = router_weight.shape[1]
    top_count = expert_ids.shape[2]
    chosen_ids = expert_ids.reshape(token_rows, top_count)
    expert_range = jnp.arange(experts, dtype=jnp.int32)
    id_marks = chosen_ids[:, :, None] == expert_range[None, None, :]
    picked = jnp.sum(jnp.where(id_marks, logits[:, None, :], 0.0), axis=2)
    scores = jax.nn.sigmoid(picked)
    gates = scores / jnp.sum(scores, axis=1, keepdims=True)
    capacity = max(2, min(token_rows, token_rows * top_count * 5 // (2 * experts)))
    flat_ids = chosen_ids.reshape(-1)
    marks = (flat_ids[:, None] == expert_range[None, :]).astype(jnp.int32)
    slots = jnp.sum((jnp.cumsum(marks, axis=0) - 1) * marks, axis=1)
    targets = flat_ids * capacity + slots
    placement = (
        jnp.arange(experts * capacity, dtype=jnp.int32)[:, None] == targets[None, :]
    ).astype(jnp.bfloat16)
    sources = jnp.repeat(normed, top_count, axis=0)
    outgoing_rows = jnp.dot(placement, sources, preferred_element_type=jnp.float32).astype(
        jnp.bfloat16
    )
    outgoing_rows = outgoing_rows.reshape(experts, capacity, model_width)
    arrived = lax.all_to_all(outgoing_rows, "expert", split_axis=0, concat_axis=0, tiled=True)
    rows = arrived.reshape(-1, model_width)
    gate_local = w_gate[0]
    up_local = w_up[0]
    down_local = w_down[0]
    partials = slice_output(
        lax.all_gather(rows, "seq", axis=0, tiled=True), gate_local, up_local, down_local
    )
    summed = lax.psum_scatter(
        partials.astype(jnp.float32).astype(jnp.bfloat16), "seq", scatter_dimension=0, tiled=True
    )
    expert_back = summed.reshape(arrived.shape)
    returned = lax.all_to_all(expert_back, "expert", split_axis=0, concat_axis=0, tiled=True)
    back_rows = lax.dot_general(
        placement,
        returned.reshape(-1, model_width),
        (((0,), (0,)), ((), ())),
        preferred_element_type=jnp.float32,
    )
    collected = back_rows.reshape(token_rows, top_count, model_width)
    routed = jnp.sum(gates[:, :, None] * collected, axis=1)
    result = (wide + routed).astype(jnp.bfloat16)
    return result.reshape(hidden_in.shape)


def solution(mesh):
    placed = (
        P(("seq", "expert"), None, None),
        P("seq", None, "expert"),
        P("seq", None, "expert"),
        P("expert", None),
        P(None, "expert"),
        P("expert"),
        P("expert", None),
        P("expert"),
        P("expert", "seq"),
        P(),
        P(),
        P(("seq", "expert"), None, None),
        P("expert", None, "seq"),
        P("expert", None, "seq"),
        P("expert", None, "seq"),
    )
    return jax.shard_map(
        body,
        mesh=mesh,
        in_specs=placed,
        out_specs=P(("seq", "expert"), None, None),
        check_vma=False,
    )
```

profile of v0, /device:TPU:2, one launch (start us, length us, event | category | flops | bytes accessed | tf_op | source)
XLA Modules:
  0.0 534.0 jit_solution(5602235171913427230)
XLA Ops:
  7.4 1.0 reshape.590
  8.4 0.9 fusion.91
  10.0 0.9 copy_convert_fusion
  10.9 96.1 %all-reduce.2.cloned.1.call-done = f32[256,288]{0,1:T(8,128)} async-done(((f32[256,288]{0,1:T(8,128)}), f32[256,288]{0,1:T(8,128)}) %all-reduce.2.cloned.1.call-update) | async-done | bytes 294928 | tf_op jit(solution)/shard_map/psum | solution.py:76
  107.0 1.4 compare_select_fusion
  109.9 11.3 %while.25 = (s32[]{:T(128)}, f32[2,256,16]{1,2,0:T(8,128)S(1)}, f32[8,16,2,256]{3,1,0,2:T(8,128)S(1)}, f32[8,16,2,256]{3,2,1,0:T(2,128)S(1)}, f32[256,16]{0,1:T(...) while((s32[]{:T(128)}, f32[2,256,16]{1,2,0:T(8,128)S(1)}, ...), condition=%wide.region_18.19_spmd.clone, body=%wide.region_1.18_spmd.clone.sunk | while | flops 1204242 | bytes 866412 | solution.py:36
  121.2 76.0 %while.24 = (s32[]{:T(128)}, f32[2,256,16]{1,2,0:T(8,128)S(1)}, f32[2,256,16]{1,2,0:T(8,128)S(1)}, f32[256,16]{0,1:T(8,128)S(1)}, f32[2,256]{1,0:T(2,128)S(1)}, /*index=5*/s32[]{:T(128)}) while((s32[]{:T(128)}, f32[2,256,16]{1,2,0:T(8,128)S(1)}, f32[2,256,16]{1,2,0:T(8,128)S(1)}, f32[256,16]{0,1:T(8,128)S(1)}, ...), condition=%wide.region_21.22_spmd.clone, body=%wide.region_20.21_spmd.clone.sunk | while | flops 24578 | bytes 247917 | solution.py:94
  121.3 1.3 collective-permute-start
  122.6 0.8 collective-permute-done
  123.4 4.4 collective-permute-start
  127.8 0.8 collective-permute-done
  128.7 4.4 collective-permute-start
  133.1 0.8 collective-permute-done
  133.9 4.4 collective-permute-start
  138.3 0.8 collective-permute-done
  139.2 4.4 collective-permute-start
  143.6 0.8 collective-permute-done
  144.4 4.4 collective-permute-start
  148.8 0.8 collective-permute-done
  149.7 4.4 collective-permute-start
  154.1 0.8 collective-permute-done
  154.9 4.4 collective-permute-start
  159.3 0.8 collective-permute-done
  160.2 4.4 collective-permute-start
  164.6 0.8 collective-permute-done
  165.4 4.4 collective-permute-start
  169.8 0.8 collective-permute-done
  170.7 4.4 collective-permute-start
  175.1 0.8 collective-permute-done
  175.9 4.4 collective-permute-start
  180.3 0.8 collective-permute-done
  181.2 4.4 collective-permute-start
  185.6 0.8 collective-permute-done
  186.4 4.4 collective-permute-start
  191.7 4.7 collective-permute-start
  197.2 1.5 multiply_reduce_fusion.16
  198.9 4.2 fusion.70
  204.3 102.3 %reduce-scatter.3.cloned.1.call-done = f32[8,2,4096]{2,0,1:T(8,128)} async-done(((f32[128,2,4096]{2,0,1:T(8,128)}), f32[8,2,4096]{2,0,1:T(8,128)}) %reduce-scatter.3.cloned.1.call-update) | async-done | bytes 262160 | tf_op jit(solution)/shard_map/reduce_scatter | solution.py:111
  306.6 1.0 add_convert_fusion
  309.0 19.8 %all_to_all.10 = bf16[16,5,4096]{2,1,0:T(8,128)(2,1)S(1)} all-to-all(bf16[16,5,4096]{2,1,0:T(8,128)(2,1)S(1)} %reshape.595), channel_id=1, replica_groups=mesh['seq'=16,'expert'=16] {'expert'}, dimensions={0} | all-to-all | bytes 1310720 | tf_op jit(solution)/shard_map/all_to_all | solution.py:148
  328.9 1.1 reshape.596
  330.3 64.0 %all-gather.5.cloned.1.call-done = bf16[1280,4096]{1,0:T(8,128)(2,1)} async-done(((bf16[80,4096]{1,0:T(8,128)(2,1)}), bf16[1280,4096]{1,0:T(8,128)(2,1)}) %all-gather.5.cloned.1.call-update) | async-done | bytes 10485776 | tf_op jit(solution)/shard_map/all_gather | solution.py:154
  394.3 11.4 %fusion.55 = f32[1280,448]{0,1:T(8,128)} fusion(bf16[1280,4096]{1,0:T(8,128)(2,1)} %all-gather.5.cloned.1.call-done, bf16[1,4096,448]{1,2,0:T(8,128)(2,1)} %param.31), kind=kOutput, calls=%fused_computation.204 | convolution fusion | flops 4697620480 | bytes 16449536 | tf_op jit(solution)/shard_map/dot_general | solution.py:46
  405.7 22.8 %convolution_convert_fusion = bf16[1280,4096]{1,0:T(8,128)(2,1)} fusion(bf16[1,4096,448]{1,2,0:T(8,128)(2,1)} %param.33, bf16[1280,4096]{1,0:T(8,128)(2,1)} %all-gather.5.cloned.1.call-done, bf16[1,4096,448]{1,2,0:T(8,128)(2,1)} %param.32, f32[1280,448]{0,1:T(8,128)} %fusion.55), kind=kOutput, calls=%fused_computation.197 | convolution fusion | flops 9403924480 | bytes 30605312 | tf_op jit(solution)/shard_map/dot_general | solution.py:49
  428.8 72.9 %reduce-scatter.5.cloned.1.call-done = bf16[80,4096]{1,0:T(8,128)(2,1)} async-done(((bf16[1280,4096]{1,0:T(8,128)(2,1)}), bf16[80,4096]{1,0:T(8,128)(2,1)}) %reduce-scatter.5.cloned.1.call-update) | async-done | bytes 655376 | tf_op jit(solution)/shard_map/reduce_scatter | solution.py:156
  501.6 2.3 reshape.597
  504.0 7.2 %all-to-all-start.1 = ((bf16[16,5,4096]{2,1,0:T(8,128)(2,1)}), bf16[16,5,4096]{2,1,0:T(8,128)(2,1)S(1)}, u32[]{:S(2)}, u32[]{:S(2)}) async-start(bf16[16,5,4096]{2,1,0:T(8,128)(2,1)} %reshape.597), calls=%async_computation.3 | async-start | bytes 2097152 | tf_op jit(solution)/shard_map/all_to_all | solution.py:160
  511.6 13.5 %all-to-all-done.1 = bf16[16,5,4096]{2,1,0:T(8,128)(2,1)S(1)} async-done(((bf16[16,5,4096]{2,1,0:T(8,128)(2,1)}), bf16[16,5,4096]{2,1,0:T(8,128)(2,1)S(1)}, u32[]{:S(2)}, u32[]{:S(2)}) %all-to-all-start.1) | async-done | bytes 655392 | tf_op jit(solution)/shard_map/all_to_all | solution.py:160
  (293 shorter events, 19.2 us)
Async XLA Ops:
  7.4 1.0 copy-start
  7.4 102.5 %copy-start.1 = (f32[256,16]{0,1:T(8,128)S(1)}, f32[256,16]{0,1:T(8,128)}, u32[]{:S(2)}) copy-start(f32[256,16]{0,1:T(8,128)} %param.25) | copy-start | bytes 49156
  7.4 99.6 %all-reduce.2.cloned.1.call-start = ((), (), s32[]{:S(2)}) async-start(), calls=%async_computation.4 | async-start | bytes 589824 | tf_op jit(solution)/shard_map/psum | solution.py:76
  9.3 189.6 %all-gather.3.cloned.1.call-start = ((), (), s32[]{:S(2)}) async-start(), calls=%async_computation.5 | async-start | bytes 2228224 | tf_op jit(solution)/shard_map/all_gather | solution.py:102
  9.9 296.7 %reduce-scatter.3.cloned.1.call-start = ((), (), s32[]{:S(2)}) async-start(), calls=%async_computation.6 | async-start | bytes 4456448 | tf_op jit(solution)/shard_map/reduce_scatter | solution.py:111
  109.9 88.8 %copy-start.2 = (bf16[128,2,256]{2,1,0:T(2,128)(2,1)S(1)}, bf16[128,2,256]{2,1,0:T(2,128)(2,1)}, u32[]{:S(2)}) copy-start(bf16[128,2,256]{2,1,0:T(2,128)(2,1)} %param.20) | copy-start | bytes 393220
  109.9 88.8 %copy-start.4 = (bf16[128,2,256]{2,1,0:T(2,128)(2,1)S(1)}, bf16[128,2,256]{2,1,0:T(2,128)(2,1)}, u32[]{:S(2)}) copy-start(bf16[128,2,256]{2,1,0:T(2,128)(2,1)} %param.21) | copy-start | bytes 393220
  109.9 88.8 %copy-start.8 = (f32[256]{0:T(256)S(1)}, f32[256]{0:T(256)}, u32[]{:S(2)}) copy-start(f32[256]{0:T(256)} %param.26) | copy-start | bytes 3076
  121.3 2.1 collective-permute-start
  123.4 5.2 collective-permute-start
  128.7 5.2 collective-permute-start
  133.9 5.2 collective-permute-start
  139.2 5.2 collective-permute-start
  144.4 5.2 collective-permute-start
  149.7 5.2 collective-permute-start
  154.9 5.2 collective-permute-start
  160.2 5.2 collective-permute-start
  165.4 5.2 collective-permute-start
  170.7 5.2 collective-permute-start
  175.9 5.2 collective-permute-start
  181.2 5.2 collective-permute-start
  186.4 5.2 collective-permute-start
  191.7 5.5 %collective-permute-start = (f32[2,256,16]{1,2,0:T(8,128)S(1)}, f32[2,256,16]{1,2,0:T(8,128)S(1)}, u32[]{:S(2)}, u32[]{:S(2)}) collective-permute-start(f32[2,256,16]{1,2,0:T(8,128)S(1)} %fusion.106), channel_id=1, source_target_pairs={{0,16},{16,32},{32,48},{48,64},{64,80},{80,96},{96,112},{112,128},... | collective-permute-start | bytes 98312 | tf_op jit(solution)/shard_map/while/body/eval_jaxpr/ppermute | solution.py:12
  203.1 0.7 copy-start.7
  203.1 103.5 %copy-start.5 = (bf16[8,2,4096]{2,1,0:T(2,128)(2,1)S(1)}, bf16[8,2,4096]{2,1,0:T(2,128)(2,1)}, u32[]{:S(2)}) copy-start(bf16[8,2,4096]{2,1,0:T(2,128)(2,1)} %param.19) | copy-start | bytes 393220
  203.1 104.9 %copy-start.6 = (f32[4096]{0:T(1024)S(1)}, f32[4096]{0:T(1024)}, u32[]{:S(2)}) copy-start(f32[4096]{0:T(1024)} %param.28) | copy-start | bytes 49156
  203.2 191.1 %all-gather.5.cloned.1.call-start = ((), (), s32[]{:S(2)}) async-start(), calls=%async_computation.7 | async-start | bytes 11141120 | tf_op jit(solution)/shard_map/all_gather | solution.py:154
  330.0 171.6 %reduce-scatter.5.cloned.1.call-start = ((), (), s32[]{:S(2)}) async-start(), calls=%async_computation.8 | async-start | bytes 11141120 | tf_op jit(solution)/shard_map/reduce_scatter | solution.py:156
  428.5 82.7 %copy-start.3 = (bf16[4096,16]{0,1:T(8,128)(2,1)S(1)}, bf16[4096,16]{0,1:T(8,128)(2,1)}, u32[]{:S(2)}) copy-start(bf16[4096,16]{0,1:T(8,128)(2,1)} %param.29) | copy-start | bytes 393220
  504.0 21.1 %all-to-all-start.1 = ((bf16[16,5,4096]{2,1,0:T(8,128)(2,1)}), bf16[16,5,4096]{2,1,0:T(8,128)(2,1)S(1)}, u32[]{:S(2)}, u32[]{:S(2)}) async-start(bf16[16,5,4096]{2,1,0:T(8,128)(2,1)} %reshape.597), calls=%async_computation.3 | async-start | bytes 2097152 | tf_op jit(solution)/shard_map/all_to_all | solution.py:160
Sparse Core Ops, SparseCore 0:
  11.4 95.5 all-reduce.1
  203.3 103.2 reduce-scatter.2
Sparse Core Ops, SparseCore 1:
  11.6 44.0 all-gather.2
  330.1 64.1 all-gather.4
  428.6 73.0 reduce-scatter.4
where the time goes:
time: 535 us; the launch traced here: 534 us
  waiting for transfers between devices  362 us (68%)
  starting transfers between devices  70.6 us (13%)
  matrix products  41.4 us (8%)
  blocking collectives  19.8 us (4%)
  between operations  15.3 us (3%)
  other arithmetic  12 us (2%)
  local copies, waits for them, and re-layouts  11.8 us (2%)
    reduce_scatter x1, waiting for transfers between devices, body(): lax.psum_scatter(product.reshape(own_rows * lax.axis_size('expert'), docs...  102 us
    psum x1, waiting for transfers between devices, body(): lax.psum(jnp.dot(flat_x, x_proj, preferred_element_type=jnp.float32), 'ex...  96.1 us
    reduce_scatter x1, waiting for transfers between devices, body(): lax.psum_scatter(partials.astype(jnp.float32).astype(jnp.bfloat16), 'seq'...  72.9 us
    all_gather x1, waiting for transfers between devices, body(): lax.all_gather(rows, 'seq', axis=0, tiled=True)  64 us
    ppermute x15, starting transfers between devices, passed_along(): return lax.ppermute(block, axis, route)  63 us
    dot_general x1, matrix products, slice_output(): lax.dot_general(hidden, down_part, (((1,), (1,)), ((), ())), preferred_el...  22.8 us
    all_to_all x1, blocking collectives, body(): lax.all_to_all(outgoing_rows, 'expert', split_axis=0, concat_axis=0, tile...  19.8 us
    all_to_all x1, waiting for transfers between devices, body(): lax.all_to_all(expert_back, 'expert', split_axis=0, concat_axis=0, tiled=...  13.5 us
  transfers between devices with their start and end apart: 21, of which 20 were waited for; matrix products, arithmetic and copies ran while one was open for 3% of the time, Pallas kernels for 0%

commit v1 on v0

v1 whole, which is shorter than its diff:
```python
import functools

import jax
import jax.numpy as jnp
from jax import lax
from jax.experimental import pallas as pl
from jax.experimental.pallas import tpu as pltpu
from jax.sharding import PartitionSpec as P

EPS = 1e-05
F32 = jnp.float32
BF16 = jnp.bfloat16
BLOCK = 16
VMEM = pl.BlockSpec(memory_space=pltpu.VMEM)
HBM = pl.BlockSpec(memory_space=pl.ANY)


def remote(src, dst, send, recv, where):
    return pltpu.make_async_remote_copy(
        src_ref=src,
        dst_ref=dst,
        send_sem=send,
        recv_sem=recv,
        device_id=where,
        device_id_type=pl.DeviceIdType.MESH,
    )


def greet(ns, ne, seq, expert):
    barrier = pltpu.get_barrier_semaphore()

    def to_seq(o, _):
        pl.semaphore_signal(
            barrier, inc=1, device_id={"seq": lax.rem(seq + o, ns)}, device_id_type=pl.DeviceIdType.MESH
        )
        return 0

    def to_expert(o, _):
        pl.semaphore_signal(
            barrier, inc=1, device_id={"expert": lax.rem(expert + o, ne)}, device_id_type=pl.DeviceIdType.MESH
        )
        return 0

    lax.fori_loop(1, ns, to_seq, 0)
    lax.fori_loop(1, ne, to_expert, 0)
    pl.semaphore_wait(barrier, ns + ne - 2)


def mixer_kernel(
    ns, ne,
    x_ref, z_ref, xp_ref, dtw_ref, dtb_ref, rates_ref, skip_ref, w_ref, hid_ref, wg_ref, wu_ref, wd_ref,
    mixed_ref, wg2_ref, wu2_ref, wd2_ref,
    part, part_in, part_sum, proj, sizes, running, reading, bc, state, state_in, gated, wf, product, product_in, total,
    pair_send, pair_recv, p1_send, p1_recv, p2_send, p2_recv, s_send, s_recv, ring_send, ring_recv,
    sib_send, sib_recv, o_send, o_recv,
):
    seq, expert = lax.axis_index("seq"), lax.axis_index("expert")
    nz = ns // 2
    hops, back = nz // 2, nz - 1 - nz // 2
    plane, core = seq // 2, lax.rem(seq, 2)
    right = lax.rem(plane + 1, nz) * 2 + core
    left = lax.rem(plane + nz - 1, nz) * 2 + core
    sibling = plane * 2 + 1 - core
    rank = dtw_ref.shape[0]
    tokens, channels = x_ref.shape
    state_n = rates_ref.shape[0]
    own = tokens // ne
    blocks = tokens // (2 * BLOCK)
    span = 2 * BLOCK
    columns = w_ref.shape[1]

    def ring_copy(stage, forward):
        if forward:
            index = lax.rem(plane + nz - (stage - 1), nz) * 2 + core
            return remote(wf.at[index], wf.at[index], ring_send.at[0, stage - 1], ring_recv.at[0, stage - 1], {"seq": right})
        index = lax.rem(plane + stage - 1, nz) * 2 + core
        return remote(wf.at[index], wf.at[index], ring_send.at[1, stage - 1], ring_recv.at[1, stage - 1], {"seq": left})

    def sibling_copy(index):
        return remote(wf.at[index], wf.at[index], sib_send.at[index // 2], sib_recv.at[index // 2], {"seq": sibling})

    def ring_stage(stage):
        if 1 < stage <= hops + 1:
            ring_copy(stage - 1, True).wait_recv()
            sibling_copy(lax.rem(plane + nz - (stage - 1), nz) * 2 + core).start()
        if 1 < stage <= back + 1:
            ring_copy(stage - 1, False).wait_recv()
            sibling_copy(lax.rem(plane + stage - 1, nz) * 2 + core).start()
        if stage <= hops:
            ring_copy(stage, True).start()
        if stage <= back:
            ring_copy(stage, False).start()

    with jax.named_scope("greet"):
        wf[seq] = w_ref[...]
        greet(ns, ne, seq, expert)
        ring_stage(1)
        sibling_copy(seq).start()
        weight_copies = [
            remote(src, dst, pair_send.at[i], pair_recv.at[i], {"seq": sibling})
            for i, (src, dst) in enumerate(((wg_ref, wg2_ref), (wu_ref, wu2_ref), (wd_ref, wd2_ref)))
        ]
        for copy in weight_copies:
            copy.start()

    with jax.named_scope("proj"):
        partial = jnp.dot(x_ref[...], xp_ref[...], preferred_element_type=F32).astype(BF16)
        part[...] = partial.reshape(part.shape)

        def part_copy(o):
            to = lax.rem(expert + o, ne)
            return remote(part.at[to], part_in.at[o - 1], p1_send.at[o - 1], p1_recv.at[o - 1], {"expert": to})

        def start_part(o, _):
            part_copy(o).start()
            return 0

        lax.fori_loop(1, ne, start_part, 0)
        ring_stage(2)

        def add_part(o, acc):
            part_copy(o).wait_recv()
            return acc + part_in[o - 1].astype(F32)

        summed = lax.fori_loop(1, ne, add_part, part[expert].astype(F32))
        part_sum[...] = summed.astype(BF16)
        proj[expert] = part_sum[...]

        def proj_copy(o):
            to = lax.rem(expert + o, ne)
            return remote(part_sum, proj.at[expert], p2_send.at[o - 1], p2_recv.at[o - 1], {"expert": to})

        def start_proj(o, _):
            proj_copy(o).start()
            return 0

        def wait_proj(o, _):
            proj_copy(o).wait_recv()
            return 0

        lax.fori_loop(1, ne, start_proj, 0)
        ring_stage(3)
        lax.fori_loop(1, ne, wait_proj, 0)

    with jax.named_scope("sizes"):
        low = proj[:, :, :rank].reshape(tokens, rank)
        raw = jnp.dot(low, dtw_ref[...], preferred_element_type=F32) + dtb_ref[...]
        sizes[...] = jnp.maximum(raw, 0.0) + jnp.log1p(jnp.exp(-jnp.abs(raw)))
        turned = proj[:, :, rank:].reshape(tokens, proj.shape[2] - rank).astype(F32).T
        for b in range(blocks):
            bc[b, :, :span] = turned[: 2 * state_n, b * span : (b + 1) * span]

    with jax.named_scope("scan"):
        rates = -rates_ref[...]
        zero_state = jnp.zeros((state_n, channels), F32)
        zero_row = jnp.zeros((1, channels), F32)

        def scan_block(b, carry):
            states, sums = [carry[0], carry[1]], [carry[2], carry[3]]
            first = pl.multiple_of(b * span, span)
            size_block = sizes[pl.ds(first, span), :]
            drive_block = size_block * x_ref[pl.ds(first, span), :].astype(F32)
            terms = bc[b]
            for r in range(span):
                d = r % 2
                size = size_block[r : r + 1]
                states[d] = (
                    jnp.exp(size * rates) * states[d] + drive_block[r : r + 1] * terms[:state_n, r : r + 1]
                )
                reading[pl.ds(first + r, 1), :] = jnp.sum(
                    states[d] * terms[state_n : 2 * state_n, r : r + 1], axis=0, keepdims=True
                )
                sums[d] = sums[d] + size
                running[pl.ds(first + r, 1), :] = sums[d]
            return states[0], states[1], sums[0], sums[1]

        end0, end1, sum0, sum1 = lax.fori_loop(
            0, blocks, scan_block, (zero_state, zero_state, zero_row, zero_row)
        )
        state[:state_n, :] = end0
        state[state_n : 2 * state_n, :] = end1
        state[2 * state_n : 2 * state_n + 8, :] = jnp.concatenate(
            [sum0, sum1, jnp.zeros((6, channels), F32)], axis=0
        )

    with jax.named_scope("states"):

        def state_copy(to, source):
            return remote(state, state_in.at[source], s_send.at[to], s_recv.at[source], {"seq": to})

        def start_state(to, _):
            state_copy(to, seq).start()
            return 0

        lax.fori_loop(seq + 1, ns, start_state, 0)
        for stage in range(4, hops + 2):
            ring_stage(stage)

        def combine(source, carry):
            state_copy(seq, source).wait_recv()
            message = state_in[source]
            through0 = jnp.exp(message[2 * state_n : 2 * state_n + 1] * rates)
            through1 = jnp.exp(message[2 * state_n + 1 : 2 * state_n + 2] * rates)
            return (
                through0 * carry[0] + message[:state_n],
                through1 * carry[1] + message[state_n : 2 * state_n],
            )

        incoming = lax.fori_loop(0, seq, combine, (zero_state, zero_state))

    with jax.named_scope("gate"):
        skip = skip_ref[...]

        def gate_block(b, _):
            first = pl.multiple_of(b * span, span)
            sum_block = running[pl.ds(first, span), :]
            terms = bc[b]
            for r in range(span):
                carried = jnp.exp(sum_block[r : r + 1] * rates) * incoming[r % 2]
                reading[pl.ds(first + r, 1), :] += jnp.sum(
                    carried * terms[state_n : 2 * state_n, r : r + 1], axis=0, keepdims=True
                )
            drive = x_ref[pl.ds(first, span), :].astype(F32)
            gate = z_ref[pl.ds(first, span), :].astype(F32)
            value = (reading[pl.ds(first, span), :] + skip * drive) * (gate / (1.0 + jnp.exp(-gate)))
            gated[pl.ds(first, span), :] = value.astype(BF16)
            return 0

        lax.fori_loop(0, blocks, gate_block, 0)

    with jax.named_scope("project"):

        def sibling_wait(i, _):
            sibling_copy(2 * i + 1 - core).wait_recv()
            return 0

        lax.fori_loop(0, nz, sibling_wait, 0)

        def multiply(b, _):
            at = pl.multiple_of(b * columns, columns)
            out = jnp.dot(gated[...], wf[b], preferred_element_type=F32).astype(BF16)
            product[:, :, pl.ds(at, columns)] = out.reshape(ne, own, columns)
            return 0

        lax.fori_loop(0, ns, multiply, 0)

        def product_copy(o):
            to = lax.rem(expert + o, ne)
            return remote(product.at[to], product_in.at[o - 1], o_send.at[o - 1], o_recv.at[o - 1], {"expert": to})

        def start_product(o, _):
            product_copy(o).start()
            return 0

        lax.fori_loop(1, ne, start_product, 0)
        total[...] = hid_ref[...].astype(F32) + product[expert].astype(F32)

        def add_product(o, _):
            product_copy(o).wait_recv()
            total[...] += product_in[o - 1].astype(F32)
            return 0

        lax.fori_loop(1, ne, add_product, 0)
        mixed_ref[...] = total[...].astype(BF16)

    with jax.named_scope("finish"):

        def sent_peers(o, _):
            part_copy(o).wait_send()
            proj_copy(o).wait_send()
            product_copy(o).wait_send()
            return 0

        lax.fori_loop(1, ne, sent_peers, 0)

        def sent_state(to, _):
            state_copy(to, seq).wait_send()
            return 0

        lax.fori_loop(seq + 1, ns, sent_state, 0)
        for stage in range(1, hops + 1):
            ring_copy(stage, True).wait_send()
        for stage in range(1, back + 1):
            ring_copy(stage, False).wait_send()

        def sent_sibling(i, _):
            sibling_copy(2 * i + core).wait_send()
            return 0

        lax.fori_loop(0, nz, sent_sibling, 0)
        for copy in weight_copies:
            copy.wait()


def mixer_call(ns, ne, x, z, xp, dtw, dtb, rates, skip, w, hid, wg, wu, wd):
    tokens, channels = x.shape
    own, width = hid.shape
    state_n = rates.shape[0]
    lanes = xp.shape[1]
    nz = ns // 2
    hops = nz // 2
    dma = pltpu.SemaphoreType.DMA
    return pl.pallas_call(
        functools.partial(mixer_kernel, ns, ne),
        out_shape=(
            jax.ShapeDtypeStruct((own, width), BF16),
            jax.ShapeDtypeStruct(wg.shape, BF16),
            jax.ShapeDtypeStruct(wu.shape, BF16),
            jax.ShapeDtypeStruct(wd.shape, BF16),
        ),
        in_specs=[VMEM] * 9 + [HBM] * 3,
        out_specs=(VMEM, HBM, HBM, HBM),
        scratch_shapes=[
            pltpu.VMEM((ne, own, lanes), BF16),
            pltpu.VMEM((ne - 1, own, lanes), BF16),
            pltpu.VMEM((own, lanes), BF16),
            pltpu.VMEM((ne, own, lanes), BF16),
            pltpu.VMEM((tokens, channels), F32),
            pltpu.VMEM((tokens, channels), F32),
            pltpu.VMEM((tokens, channels), F32),
            pltpu.VMEM((tokens // (2 * BLOCK), 2 * state_n, 128), F32),
            pltpu.VMEM((2 * state_n + 8, channels), F32),
            pltpu.VMEM((ns, 2 * state_n + 8, channels), F32),
            pltpu.VMEM((tokens, channels), BF16),
            pltpu.VMEM((ns,) + w.shape, BF16),
            pltpu.VMEM((ne, own, width), BF16),
            pltpu.VMEM((ne - 1, own, width), BF16),
            pltpu.VMEM((own, width), F32),
            dma((3,)), dma((3,)),
            dma((ne - 1,)), dma((ne - 1,)),
            dma((ne - 1,)), dma((ne - 1,)),
            dma((ns,)), dma((ns,)),
            dma((2, hops)), dma((2, hops)),
            dma((nz,)), dma((nz,)),
            dma((ne - 1,)), dma((ne - 1,)),
        ],
        compiler_params=pltpu.CompilerParams(
            collective_id=0, has_side_effects=True, vmem_limit_bytes=48 * 1024 * 1024
        ),
    )(x, z, xp, dtw, dtb, rates, skip, w, hid, wg, wu, wd)


def expert_kernel(
    ns,
    rows_ref, wg_ref, wu_ref, wd_ref, wg2_ref, wu2_ref, wd2_ref,
    out_ref,
    held, parts, from_left, from_right, gate_w, up_w, down_w, hidden,
    w_sem, g_send, g_recv, r_send, r_recv,
):
    seq = lax.axis_index("seq")
    nz = ns // 2
    hops = nz // 2
    plane, core = seq // 2, lax.rem(seq, 2)
    right = {"seq": lax.rem(plane + 1, nz) * 2 + core}
    left = {"seq": lax.rem(plane + nz - 1, nz) * 2 + core}
    count, width = rows_ref.shape
    half = width // 2
    low, high = pl.ds(0, half), pl.ds(half, half)

    def gather_copy(stage, forward):
        side = 0 if forward else 1
        source = held.at[2 * (stage - 1) + (0 if forward or stage == 1 else 1)]
        if stage < hops:
            target = held.at[2 * stage + side]
        else:
            columns = low if forward else high
            source, target = source.at[:, columns], held.at[1, :, columns]
        return remote(
            source, target, g_send.at[side, stage - 1], g_recv.at[side, stage - 1], right if forward else left
        )

    def return_copy(stage, forward):
        side = 0 if forward else 1
        buffer = from_left if forward else from_right
        distance = hops - stage + 1
        if stage == 1:
            columns = low if forward else high
            source, target = parts.at[1, :, columns], buffer.at[0, :, columns]
        else:
            source, target = parts.at[2 * distance + (1 if forward else 0)], buffer.at[stage - 1]
        return remote(
            source, target, r_send.at[side, stage - 1], r_recv.at[side, stage - 1], right if forward else left
        )

    with jax.named_scope("load"):
        loads = [
            pltpu.make_async_copy(src, dst.at[i], w_sem.at[j, i])
            for j, (pair, dst) in enumerate(
                (((wg_ref, wg2_ref), gate_w), ((wu_ref, wu2_ref), up_w), ((wd_ref, wd2_ref), down_w))
            )
            for i, src in enumerate(pair)
        ]
        for copy in loads:
            copy.start()
        held[0] = rows_ref[...]
        barrier = pltpu.get_barrier_semaphore()
        for to in (left, right):
            pl.semaphore_signal(barrier, inc=1, device_id=to, device_id_type=pl.DeviceIdType.MESH)
        pl.semaphore_wait(barrier, 2)
        gather_copy(1, True).start()
        gather_copy(1, False).start()

    def compute(pair):
        rows = held[2 * pair : 2 * pair + 2].reshape(2 * count, width)
        for i in range(2):
            gate = jnp.dot(rows, gate_w[i], preferred_element_type=F32)
            up = jnp.dot(rows, up_w[i], preferred_element_type=F32)
            hidden[i] = (gate / (1.0 + jnp.exp(-gate)) * up).astype(BF16)
        step = min(width, 512)

        def down(b, _):
            at = pl.multiple_of(b * step, step)
            out = sum(
                lax.dot_general(
                    hidden[i], down_w[i, pl.ds(at, step), :], (((1,), (1,)), ((), ())), preferred_element_type=F32
                )
                for i in range(2)
            )
            parts[2 * pair : 2 * pair + 2, :, pl.ds(at, step)] = out.astype(BF16).reshape(2, count, step)
            return 0

        lax.fori_loop(0, width // step, down, 0)

    for stage in range(1, hops + 1):
        with jax.named_scope("gather"):
            gather_copy(stage, True).wait_recv()
            gather_copy(stage, False).wait_recv()
            if stage < hops:
                gather_copy(stage + 1, True).start()
                gather_copy(stage + 1, False).start()
            if stage == 1:
                for copy in loads:
                    copy.wait()
        with jax.named_scope("experts"):
            compute(stage if stage < hops else 0)

    for stage in range(1, hops + 1):
        with jax.named_scope("combine"):
            if stage > 1:
                distance = hops - stage + 1
                for forward, buffer in ((True, from_left), (False, from_right)):
                    return_copy(stage - 1, forward).wait_recv()
                    slot = 2 * distance + (1 if forward else 0)
                    if stage == 2:
                        columns = low if forward else high
                        parts[slot, :, columns] = (
                            parts[slot, :, columns].astype(F32) + buffer[0, :, columns].astype(F32)
                        ).astype(BF16)
                    else:
                        parts[slot] = (parts[slot].astype(F32) + buffer[stage - 2].astype(F32)).astype(BF16)
                    return_copy(stage, forward).start()
            else:
                return_copy(1, True).start()
                return_copy(1, False).start()

    with jax.named_scope("last"):
        return_copy(hops, True).wait_recv()
        return_copy(hops, False).wait_recv()
        if hops > 1:
            total = from_left[hops - 1].astype(F32) + from_right[hops - 1].astype(F32)
            out_ref[...] = (parts[0].astype(F32) + total).astype(BF16)
        else:
            out_ref[:, low] = (parts[0, :, low].astype(F32) + from_left[0, :, low].astype(F32)).astype(BF16)
            out_ref[:, high] = (parts[0, :, high].astype(F32) + from_right[0, :, high].astype(F32)).astype(BF16)
        for stage in range(1, hops + 1):
            for forward in (True, False):
                gather_copy(stage, forward).wait_send()
                return_copy(stage, forward).wait_send()


def expert_call(ns, rows, wg, wu, wd, wg2, wu2, wd2):
    count, width = rows.shape
    hid = wg.shape[1]
    nz = ns // 2
    hops = nz // 2
    dma = pltpu.SemaphoreType.DMA
    return pl.pallas_call(
        functools.partial(expert_kernel, ns),
        out_shape=jax.ShapeDtypeStruct((count, width), BF16),
        in_specs=[VMEM] + [HBM] * 6,
        out_specs=VMEM,
        scratch_shapes=[
            pltpu.VMEM((nz, count, width), BF16),
            pltpu.VMEM((nz, count, width), BF16),
            pltpu.VMEM((hops, count, width), BF16),
            pltpu.VMEM((hops, count, width), BF16),
            pltpu.VMEM((2, width, hid), BF16),
            pltpu.VMEM((2, width, hid), BF16),
            pltpu.VMEM((2, width, hid), BF16),
            pltpu.VMEM((2, 2 * count, hid), BF16),
            dma((3, 2)),
            dma((2, hops)), dma((2, hops)),
            dma((2, hops)), dma((2, hops)),
        ],
        compiler_params=pltpu.CompilerParams(
            collective_id=1, has_side_effects=True, vmem_limit_bytes=60 * 1024 * 1024
        ),
    )(rows, wg, wu, wd, wg2, wu2, wd2)


def body(
    hidden_in,
    mamba_x,
    mamba_z,
    x_proj,
    dt_weight,
    dt_bias,
    state_rates,
    skip_gain,
    out_weight,
    norm_gain,
    router_weight,
    expert_ids,
    w_gate,
    w_up,
    w_down,
):
    ns, ne = lax.axis_size("seq"), lax.axis_size("expert")
    slice_len, docs, channels = mamba_x.shape
    model_width = hidden_in.shape[2]
    token_rows = hidden_in.shape[0] * docs
    lanes = -(-x_proj.shape[1] // 128) * 128
    mixed, wg2, wu2, wd2 = mixer_call(
        ns,
        ne,
        mamba_x.reshape(slice_len * docs, channels),
        mamba_z.reshape(slice_len * docs, channels),
        jnp.pad(x_proj, ((0, 0), (0, lanes - x_proj.shape[1]))),
        dt_weight,
        dt_bias[None],
        state_rates.T,
        skip_gain[None],
        out_weight,
        hidden_in.reshape(token_rows, model_width),
        w_gate[0],
        w_up[0],
        w_down[0],
    )
    wide = mixed.astype(jnp.float32)
    normed = (
        wide * lax.rsqrt(jnp.mean(wide * wide, axis=-1, keepdims=True) + EPS) * norm_gain
    ).astype(jnp.bfloat16)
    logits = jnp.dot(normed, router_weight, preferred_element_type=jnp.float32)
    experts = router_weight.shape[1]
    top_count = expert_ids.shape[2]
    chosen_ids = expert_ids.reshape(token_rows, top_count)
    expert_range = jnp.arange(experts, dtype=jnp.int32)
    id_marks = chosen_ids[:, :, None] == expert_range[None, None, :]
    picked = jnp.sum(jnp.where(id_marks, logits[:, None, :], 0.0), axis=2)
    scores = jax.nn.sigmoid(picked)
    gates = scores / jnp.sum(scores, axis=1, keepdims=True)
    capacity = max(2, min(token_rows, token_rows * top_count * 5 // (2 * experts)))
    flat_ids = chosen_ids.reshape(-1)
    marks = (flat_ids[:, None] == expert_range[None, :]).astype(jnp.int32)
    slots = jnp.sum((jnp.cumsum(marks, axis=0) - 1) * marks, axis=1)
    targets = flat_ids * capacity + slots
    placement = (
        jnp.arange(experts * capacity, dtype=jnp.int32)[:, None] == targets[None, :]
    ).astype(jnp.bfloat16)
    sources = jnp.repeat(normed, top_count, axis=0)
    outgoing_rows = jnp.dot(placement, sources, preferred_element_type=jnp.float32).astype(
        jnp.bfloat16
    )
    outgoing_rows = outgoing_rows.reshape(experts, capacity, model_width)
    arrived = lax.all_to_all(outgoing_rows, "expert", split_axis=0, concat_axis=0, tiled=True)
    rows = arrived.reshape(-1, model_width)
    summed = expert_call(ns, rows, w_gate[0], w_up[0], w_down[0], wg2, wu2, wd2)
    expert_back = summed.reshape(arrived.shape)
    returned = lax.all_to_all(expert_back, "expert", split_axis=0, concat_axis=0, tiled=True)
    back_rows = lax.dot_general(
        placement,
        returned.reshape(-1, model_width),
        (((0,), (0,)), ((), ())),
        preferred_element_type=jnp.float32,
    )
    collected = back_rows.reshape(token_rows, top_count, model_width)
    routed = jnp.sum(gates[:, :, None] * collected, axis=1)
    result = (wide + routed).astype(jnp.bfloat16)
    return result.reshape(hidden_in.shape)


def solution(mesh):
    placed = (
        P(("seq", "expert"), None, None),
        P("seq", None, "expert"),
        P("seq", None, "expert"),
        P("expert", None),
        P(None, "expert"),
        P("expert"),
        P("expert", None),
        P("expert"),
        P("expert", "seq"),
        P(),
        P(),
        P(("seq", "expert"), None, None),
        P("expert", None, "seq"),
        P("expert", None, "seq"),
        P("expert", None, "seq"),
    )
    return jax.shard_map(
        body,
        mesh=mesh,
        in_specs=placed,
        out_specs=P(("seq", "expert"), None, None),
        check_vma=False,
    )
```

time: 535 us -> 269 us (0.50)
  waiting for transfers between devices: 362 us -> 27.7 us
  Pallas kernels: 0 us -> 189 us
  starting transfers between devices: 70.6 us -> 17 us
  matrix products: 41.4 us -> 0.68 us
  local copies, waits for them, and re-layouts: 11.8 us -> 32.7 us
  blocking collectives: 19.8 us -> 0 us
  between operations: 15.3 us -> 0.21 us
  other arithmetic: 12 us -> 0.88 us
    pallas_call x0 -> x2, Pallas kernels: none -> 189 us  [the longest x1 122 us: expert_call(): pl.pallas_call(functools.partial(expert_kernel, ns), out_shape=jax.ShapeD...]
    reduce_scatter x2 -> x0, waiting for transfers between devices: 175 us -> none  [the longest x1 102 us: body(): lax.psum_scatter(product.reshape(own_rows * lax.axis_size('expert'), docs...]
    psum x1 -> x0, waiting for transfers between devices: 96.1 us -> none  [body(): lax.psum(jnp.dot(flat_x, x_proj, preferred_element_type=jnp.float32), 'ex...]
    all_gather x2 -> x0, waiting for transfers between devices: 64.1 us -> none  [the longest x1 64 us: body(): lax.all_gather(rows, 'seq', axis=0, tiled=True)]
    ppermute x15 -> x0, starting transfers between devices: 63 us -> none  [passed_along(): return lax.ppermute(block, axis, route)]
    dot_general x5 -> x0, matrix products: 40.7 us -> none  [the longest x1 22.8 us: slice_output(): lax.dot_general(hidden, down_part, (((1,), (1,)), ((), ())), preferred_el...]
    unnamed x20 -> x24, local copies, waits for them, and re-layouts: 0.82 us -> 23.4 us
    all_to_all x1 -> x0, blocking collectives: 19.8 us -> none  [body(): lax.all_to_all(outgoing_rows, 'expert', split_axis=0, concat_axis=0, tile...]
  transfers between devices with their start and end apart: 21 -> 2, of which waited for: 20 -> 2; matrix products, arithmetic and copies ran while one was open for 3% -> 0% of each run, Pallas kernels for 0% -> 0%
where the time goes in v1:
time: 269 us; the launch traced here: 268 us
  Pallas kernels  189 us (70%)
  local copies, waits for them, and re-layouts  32.7 us (12%)
  waiting for transfers between devices  27.7 us (10%)
  starting transfers between devices  17 us (6%)
    pallas_call x1, Pallas kernels, expert_call(): pl.pallas_call(functools.partial(expert_kernel, ns), out_shape=jax.ShapeD...  122 us
    pallas_call x1, Pallas kernels, mixer_call(): pl.pallas_call(functools.partial(mixer_kernel, ns, ne), out_shape=(jax.Sh...  67 us
    unnamed x24, local copies, waits for them, and re-layouts  23.4 us
    all_to_all x1, waiting for transfers between devices, body(): lax.all_to_all(outgoing_rows, 'expert', split_axis=0, concat_axis=0, tile...  14.9 us
    all_to_all x1, waiting for transfers between devices, body(): lax.all_to_all(expert_back, 'expert', split_axis=0, concat_axis=0, tiled=...  12.9 us
    all_to_all x1, starting transfers between devices, body(): lax.all_to_all(outgoing_rows, 'expert', split_axis=0, concat_axis=0, tile...  11.2 us
    all_to_all x1, starting transfers between devices, body(): lax.all_to_all(expert_back, 'expert', split_axis=0, concat_axis=0, tiled=...  5.73 us
  transfers between devices with their start and end apart: 2, of which 2 were waited for; matrix products, arithmetic and copies ran while one was open for 0% of the time, Pallas kernels for 0%

profile of v1, /device:TPU:2, one launch (start us, length us, event | category | flops | bytes accessed | tf_op | source)
XLA Modules:
  0.0 268.0 jit_solution(17115558463958248413)
XLA Ops:
  0.0 0.0 copy-start
  0.0 0.8 copy.36
  0.8 0.1 reshape_reshape.3
  0.9 0.1 fusion.6
  1.0 0.1 reduce_window_sum.11
  1.0 0.2 select_reduce_fusion
  1.2 1.0 reshape.97.hid_ref
  2.2 1.0 reshape.95.x_ref
  3.2 1.0 reshape.96.z_ref
  4.1 1.1 copy.31
  5.2 6.4 %copy.32 = bf16[1,4096,448]{2,1,0:T(8,128)(2,1)} copy(bf16[1,4096,448]{1,2,0:T(8,128)(2,1)} %param.27) | data formatting | bytes 7340032 | tf_op args[12]
  11.6 6.5 %copy.33 = bf16[1,4096,448]{2,1,0:T(8,128)(2,1)} copy(bf16[1,4096,448]{1,2,0:T(8,128)(2,1)} %param.28) | data formatting | bytes 7340032 | tf_op args[13]
  18.1 0.0 copy-start.2
  18.1 0.0 copy-start.6
  18.1 6.5 %copy.34 = bf16[1,4096,448]{2,1,0:T(8,128)(2,1)} copy(bf16[1,4096,448]{1,2,0:T(8,128)(2,1)} %param.29) | data formatting | bytes 7340032 | tf_op args[14]
  24.7 0.0 copy-done.2
  24.7 0.0 copy-done.3
  24.7 0.0 copy-done.4
  24.7 0.0 copy-done.5
  24.7 0.0 copy-done.6
  24.7 0.0 copy-start.7
  24.8 67.0 %shard_map.145 = (bf16[16,4096]{1,0:T(8,128)(2,1)S(1)}, bf16[4096,448]{1,0:T(8,128)(2,1)S(1)}, bf16[4096,448]{1,0:T(8,128)(2,1)}, bf16[4096,448]{1,0:T(8,128)(2,1)}) custom-call(bf16[256,256]{1,0:T(8,128)(2,1)S(1)} %reshape.95.x_ref, bf16[256,256]{1,0:T(8,128)(2,1)S(1)} %reshape.96.z_ref, bf16[256,384]{1,0:T(8,128)(2,1)S(1)} %pad.4.xp_ref, ...), custom_call_target="tpu_custom_call" | custom-call | tf_op jit(solution)/shard_map/pallas_call | solution.py:303
  91.8 0.0 copy-start.1
  91.8 2.0 copy-done.1
  93.8 0.1 fusion.1
  93.9 0.0 copy-done.7
  93.9 0.1 fusion.3
  94.0 0.2 broadcast_in_dim.34
  94.2 0.1 reshape.98
  94.4 0.3 convolution_convert_fusion
  94.7 1.3 reshape.99
  96.0 11.2 %all-to-all-start = ((bf16[16,5,4096]{2,1,0:T(8,128)(2,1)}), bf16[16,5,4096]{2,1,0:T(8,128)(2,1)S(1)}, u32[]{:S(2)}, u32[]{:S(2)}) async-start(bf16[16,5,4096]{2,1,0:T(8,128)(2,1)} %reshape.99), calls=%async_computation | async-start | bytes 2097152 | tf_op jit(solution)/shard_map/all_to_all | solution.py:565
  107.2 0.0 copy-done.8
  107.2 0.1 copy.35
  107.3 0.1 eq.56
  107.4 0.1 iota_compare_fusion.3
  107.5 14.9 %all-to-all-done = bf16[16,5,4096]{2,1,0:T(8,128)(2,1)S(1)} async-done(((bf16[16,5,4096]{2,1,0:T(8,128)(2,1)}), bf16[16,5,4096]{2,1,0:T(8,128)(2,1)S(1)}, u32[]{:S(2)}, u32[]{:S(2)}) %all-to-all-start) | async-done | bytes 655392 | tf_op jit(solution)/shard_map/all_to_all | solution.py:565
  122.4 1.2 reshape.100.rows_ref
  123.5 121.8 %shard_map.146 = bf16[80,4096]{1,0:T(8,128)(2,1)} custom-call(bf16[80,4096]{1,0:T(8,128)(2,1)} %reshape.100.rows_ref, bf16[4096,448]{1,0:T(8,128)(2,1)} %bitcast.16, bf16[4096,448]{1,0:T(8,128)(2,1)} %bitcast.18, bf16[4096,448]{1,0:T(8,128)(2,1)} %bitcast.20, bf16[4096,448]{1,0:T(8,128)(2,1)} %copy-done.1, bf16[4096,448]{1,0:T(8,128)(2,1)} %get-tuple-element.11.wu2_ref, ...), custom_call_target="tpu_custom_call" | custom-call | tf_op jit(solution)/shard_map/pallas_call | solution.py:477
  245.3 2.3 reshape.101
  247.7 5.7 %all-to-all-start.1 = ((bf16[16,5,4096]{2,1,0:T(8,128)(2,1)}), bf16[16,5,4096]{2,1,0:T(8,128)(2,1)S(1)}, u32[]{:S(2)}, u32[]{:S(2)}) async-start(bf16[16,5,4096]{2,1,0:T(8,128)(2,1)} %reshape.101), calls=%async_computation.1 | async-start | bytes 2097152 | tf_op jit(solution)/shard_map/all_to_all | solution.py:569
  253.4 0.0 copy-done
  253.4 0.2 fusion.8
  253.6 0.2 select_reduce_fusion.1
  253.8 12.9 %all-to-all-done.1 = bf16[16,5,4096]{2,1,0:T(8,128)(2,1)S(1)} async-done(((bf16[16,5,4096]{2,1,0:T(8,128)(2,1)}), bf16[16,5,4096]{2,1,0:T(8,128)(2,1)S(1)}, u32[]{:S(2)}, u32[]{:S(2)}) %all-to-all-start.1) | async-done | bytes 655392 | tf_op jit(solution)/shard_map/all_to_all | solution.py:569
  266.7 0.3 reshape.104
  266.9 0.2 fusion
  267.2 0.8 reshape.103
  (11 shorter events, 0.1 us)
Async XLA Ops:
  0.0 253.4 %copy-start = (bf16[4096,16]{0,1:T(8,128)(2,1)S(1)}, bf16[4096,16]{0,1:T(8,128)(2,1)}, u32[]{:S(2)}) copy-start(bf16[4096,16]{0,1:T(8,128)(2,1)} %param.25) | copy-start | bytes 393220
  18.1 6.6 %copy-start.2 = (bf16[256,256]{1,0:T(8,128)(2,1)S(1)}, bf16[256,256]{1,0:T(8,128)(2,1)}, u32[]{:S(2)}) copy-start(bf16[256,256]{1,0:T(8,128)(2,1)} %dtw_ref.1) | copy-start | bytes 393220
  18.1 6.6 %copy-start.3 = (bf16[256,256]{1,0:T(8,128)(2,1)S(1)}, bf16[256,256]{1,0:T(8,128)(2,1)}, u32[]{:S(2)}) copy-start(bf16[256,256]{1,0:T(8,128)(2,1)} %w_ref.1) | copy-start | bytes 393220
  18.1 6.6 %copy-start.4 = (f32[256,16]{0,1:T(8,128)S(1)}, f32[256,16]{0,1:T(8,128)}, u32[]{:S(2)}) copy-start(f32[256,16]{0,1:T(8,128)} %param.21) | copy-start | bytes 49156
  18.1 6.6 %copy-start.5 = (f32[256]{0:T(256)S(1)}, f32[256]{0:T(256)}, u32[]{:S(2)}) copy-start(f32[256]{0:T(256)} %param.20) | copy-start | bytes 3076
  18.1 6.6 %copy-start.6 = (f32[256]{0:T(256)S(1)}, f32[256]{0:T(256)}, u32[]{:S(2)}) copy-start(f32[256]{0:T(256)} %param.22) | copy-start | bytes 3076
  24.7 69.2 %copy-start.7 = (f32[4096]{0:T(1024)S(1)}, f32[4096]{0:T(1024)}, u32[]{:S(2)}) copy-start(f32[4096]{0:T(1024)} %param.24) | copy-start | bytes 49156
  91.8 2.0 copy-start.1
  93.8 13.5 %copy-start.8 = (s32[8,2,2]{0,2,1:T(2,128)S(1)}, s32[8,2,2]{0,2,1:T(2,128)}, u32[]{:S(2)}) copy-start(s32[8,2,2]{0,2,1:T(2,128)} %param.26) | copy-start | bytes 388
  96.0 26.4 %all-to-all-start = ((bf16[16,5,4096]{2,1,0:T(8,128)(2,1)}), bf16[16,5,4096]{2,1,0:T(8,128)(2,1)S(1)}, u32[]{:S(2)}, u32[]{:S(2)}) async-start(bf16[16,5,4096]{2,1,0:T(8,128)(2,1)} %reshape.99), calls=%async_computation | async-start | bytes 2097152 | tf_op jit(solution)/shard_map/all_to_all | solution.py:565
  247.7 19.0 %all-to-all-start.1 = ((bf16[16,5,4096]{2,1,0:T(8,128)(2,1)}), bf16[16,5,4096]{2,1,0:T(8,128)(2,1)S(1)}, u32[]{:S(2)}, u32[]{:S(2)}) async-start(bf16[16,5,4096]{2,1,0:T(8,128)(2,1)} %reshape.101), calls=%async_computation.1 | async-start | bytes 2097152 | tf_op jit(solution)/shard_map/all_to_all | solution.py:569

commit v2 on v1

v2 whole, which is shorter than its diff:
```python
import functools

import jax
import jax.numpy as jnp
from jax import lax
from jax.experimental import pallas as pl
from jax.experimental.pallas import tpu as pltpu
from jax.sharding import PartitionSpec as P

EPS = 1e-05
F32 = jnp.float32
BF16 = jnp.bfloat16
BLOCK = 16
VMEM = pl.BlockSpec(memory_space=pltpu.VMEM)
HBM = pl.BlockSpec(memory_space=pl.ANY)


def remote(src, dst, send, recv, where):
    return pltpu.make_async_remote_copy(
        src_ref=src,
        dst_ref=dst,
        send_sem=send,
        recv_sem=recv,
        device_id=where,
        device_id_type=pl.DeviceIdType.MESH,
    )


def greet(ns, ne, seq, expert):
    barrier = pltpu.get_barrier_semaphore()

    def to_seq(o, _):
        pl.semaphore_signal(
            barrier, inc=1, device_id={"seq": lax.rem(seq + o, ns)}, device_id_type=pl.DeviceIdType.MESH
        )
        return 0

    def to_expert(o, _):
        pl.semaphore_signal(
            barrier, inc=1, device_id={"expert": lax.rem(expert + o, ne)}, device_id_type=pl.DeviceIdType.MESH
        )
        return 0

    lax.fori_loop(1, ns, to_seq, 0)
    lax.fori_loop(1, ne, to_expert, 0)
    pl.semaphore_wait(barrier, ns + ne - 2)


def layer_kernel(
    ns, ne, cap,
    x_ref, z_ref, xp_ref, dtw_ref, dtb_ref, rates_ref, skip_ref, w_ref, hid_ref,
    gain_ref, router_ref, place_ref, pick_ref, put_ref, wg_ref, wu_ref, wd_ref,
    out_ref,
    part, part_in, part_sum, proj, sizes, running, reading, bc,
    state, state_sib, state_chip, state_in, incoming, gated, wf,
    product, row_in, row_sum, row_last, col_in, col_sum, col_last,
    wide, combine_w, flat, packed_out, packed_in, back_out, back_in, returned,
    held, parts, from_left, from_right, gate_w, up_w, down_w, hidden,
    load_sem, pair_send, pair_recv, p1_send, p1_recv, p2_send, p2_recv,
    h_send, h_recv, s_send, s_recv, ring_send, ring_recv, sib_send, sib_recv,
    a_send, a_recv, b_send, b_recv, d_send, d_recv, e_send, e_recv,
    g_send, g_recv, r_send, r_recv,
):
    seq, expert = lax.axis_index("seq"), lax.axis_index("expert")
    nz = ns // 2
    hops, back = nz // 2, nz - 1 - nz // 2
    ny, nx = product.shape[0], product.shape[1]
    ey, ex = expert // nx, lax.rem(expert, nx)
    plane, core = seq // 2, lax.rem(seq, 2)
    right = lax.rem(plane + 1, nz) * 2 + core
    left = lax.rem(plane + nz - 1, nz) * 2 + core
    sibling = {"seq": plane * 2 + 1 - core}
    rank = dtw_ref.shape[0]
    tokens, channels = x_ref.shape
    state_n = rates_ref.shape[0]
    own, width = hid_ref.shape
    half = width // 2
    low, high = pl.ds(0, half), pl.ds(half, half)
    blocks = tokens // (2 * BLOCK)
    span = 2 * BLOCK
    columns = w_ref.shape[1]
    count = ne * cap
    units = wg_ref.shape[0]
    pieces = width // 128

    def loop(start, stop, action):
        def step(i, carry):
            action(i)
            return carry

        lax.fori_loop(start, stop, step, 0)

    def ring_copy(stage, forward):
        side, to = (0, right) if forward else (1, left)
        index = lax.rem(plane + (nz - stage + 1 if forward else stage - 1), nz) * 2 + core
        return remote(
            wf.at[index], wf.at[index], ring_send.at[side, stage - 1], ring_recv.at[side, stage - 1], {"seq": to}
        )

    def sibling_copy(index):
        return remote(wf.at[index], wf.at[index], sib_send.at[index // 2], sib_recv.at[index // 2], sibling)

    def ring_stage(stage):
        if 1 < stage <= hops + 1:
            ring_copy(stage - 1, True).wait_recv()
            sibling_copy(lax.rem(plane + nz - (stage - 1), nz) * 2 + core).start()
        if 1 < stage <= back + 1:
            ring_copy(stage - 1, False).wait_recv()
            sibling_copy(lax.rem(plane + stage - 1, nz) * 2 + core).start()
        if stage <= hops:
            ring_copy(stage, True).start()
        if stage <= back:
            ring_copy(stage, False).start()

    with jax.named_scope("greet"):
        weights = ((wg_ref, gate_w), (wu_ref, up_w), (wd_ref, down_w))
        loads = [
            pltpu.make_async_copy(src, dst.at[pl.ds(0, units)], load_sem.at[i])
            for i, (src, dst) in enumerate(weights)
        ]
        for copy in loads:
            copy.start()
        wf[seq] = w_ref[...]
        greet(ns, ne, seq, expert)
        ring_stage(1)
        sibling_copy(seq).start()

    with jax.named_scope("proj"):
        partial = lax.dot_general(
            x_ref[...], xp_ref[...], (((1,), (1,)), ((), ())), preferred_element_type=F32
        ).astype(BF16)
        spare = part.shape[2] - partial.shape[1]
        part[...] = jnp.concatenate([partial, jnp.zeros((tokens, spare), BF16)], axis=1).reshape(part.shape)

        def part_copy(o):
            to = lax.rem(expert + o, ne)
            return remote(part.at[to], part_in.at[o - 1], p1_send.at[o - 1], p1_recv.at[o - 1], {"expert": to})

        loop(1, ne, lambda o: part_copy(o).start())
        pairs = [
            remote(src, dst.at[pl.ds(units, units)], pair_send.at[i], pair_recv.at[i], sibling)
            for i, (src, dst) in enumerate(weights)
        ]

        def add_part(o, acc):
            part_copy(o).wait_recv()
            return acc + part_in[o - 1].astype(F32)

        summed = lax.fori_loop(1, ne, add_part, part[expert].astype(F32))
        part_sum[...] = summed.astype(BF16)
        proj[expert] = part_sum[...]

        def proj_copy(o):
            to = lax.rem(expert + o, ne)
            return remote(part_sum, proj.at[expert], p2_send.at[o - 1], p2_recv.at[o - 1], {"expert": to})

        loop(1, ne, lambda o: proj_copy(o).start())
        ring_stage(2)
        loop(1, ne, lambda o: proj_copy(o).wait_recv())

    with jax.named_scope("sizes"):
        proj_all = proj[...].reshape(tokens, proj.shape[2])
        raw = jnp.dot(proj_all[:, :rank], dtw_ref[...], preferred_element_type=F32) + dtb_ref[...]
        sizes[...] = jnp.maximum(raw, 0.0) + jnp.log1p(jnp.exp(-jnp.abs(raw)))
        turned = proj_all[:, rank:].astype(F32).T
        for b in range(blocks):
            bc[b, :, :span] = turned[: 2 * state_n, b * span : (b + 1) * span]

    with jax.named_scope("scan"):
        rates = -rates_ref[...]
        zero_state = jnp.zeros((state_n, channels), F32)
        zero_row = jnp.zeros((1, channels), F32)

        def scan_block(b, carry):
            states, sums = [carry[0], carry[1]], [carry[2], carry[3]]
            first = pl.multiple_of(b * span, span)
            size_block = sizes[pl.ds(first, span), :]
            drive_block = size_block * x_ref[pl.ds(first, span), :].astype(F32)
            terms = bc[b]
            for r in range(span):
                d = r % 2
                size = size_block[r : r + 1]
                states[d] = (
                    jnp.exp(size * rates) * states[d] + drive_block[r : r + 1] * terms[:state_n, r : r + 1]
                )
                reading[pl.ds(first + r, 1), :] = jnp.sum(
                    states[d] * terms[state_n : 2 * state_n, r : r + 1], axis=0, keepdims=True
                )
                sums[d] = sums[d] + size
                running[pl.ds(first + r, 1), :] = sums[d]
            return states[0], states[1], sums[0], sums[1]

        end0, end1, sum0, sum1 = lax.fori_loop(
            0, blocks, scan_block, (zero_state, zero_state, zero_row, zero_row)
        )
        state[:state_n, :] = end0
        state[state_n : 2 * state_n, :] = end1
        state[2 * state_n : 2 * state_n + 8, :] = jnp.concatenate(
            [sum0, sum1, jnp.zeros((6, channels), F32)], axis=0
        )

    with jax.named_scope("states"):
        side = channels // 2
        mine = pl.ds(pl.multiple_of(core * side, side), side)
        other = pl.ds(pl.multiple_of((1 - core) * side, side), side)
        half_copy = remote(state.at[:, other], state_sib, h_send.at[0], h_recv.at[0], sibling)
        half_copy.start()
        ring_stage(3)
        rates_mine = -rates_ref[:, mine]

        def through(message, d):
            return jnp.exp(message[2 * state_n + d : 2 * state_n + d + 1] * rates_mine)

        def ends(message, d):
            return message[d * state_n : (d + 1) * state_n]

        half_copy.wait_recv()
        first_core = core == 0
        here, there = state[:, mine], state_sib[...]
        early = jnp.where(first_core, here, there)
        late = jnp.where(first_core, there, here)
        for d in range(2):
            state_chip[d * state_n : (d + 1) * state_n, :] = through(late, d) * ends(early, d) + ends(late, d)
        state_chip[2 * state_n :, :] = early[2 * state_n :] + late[2 * state_n :]

        def state_copy(to, source):
            return remote(state_chip, state_in.at[source], s_send.at[to], s_recv.at[source], {"seq": to * 2 + core})

        loop(plane + 1, nz, lambda to: state_copy(to, plane).start())
        for copy in pairs:
            copy.start()

        def horner(source, carry):
            state_copy(plane, source).wait_recv()
            message = state_in[source]
            return tuple(through(message, d) * carry[d] + ends(message, d) for d in range(2))

        zero_half = jnp.zeros((state_n, side), F32)
        entering = lax.fori_loop(0, plane, horner, (zero_half, zero_half))
        for d in range(2):
            passed = through(early, d) * entering[d] + ends(early, d)
            state_sib[d * state_n : (d + 1) * state_n, :] = jnp.where(first_core, passed, entering[d])
            incoming[d * state_n : (d + 1) * state_n, mine] = jnp.where(first_core, entering[d], passed)
        enter_copy = remote(
            state_sib.at[pl.ds(0, 2 * state_n)], incoming.at[:, mine], h_send.at[1], h_recv.at[1], sibling
        )
        enter_copy.start()
        for stage in range(4, hops + 2):
            ring_stage(stage)
        enter_copy.wait_recv()

    with jax.named_scope("gate"):
        skip = skip_ref[...]
        entered = [incoming[d * state_n : (d + 1) * state_n, :] for d in range(2)]

        def gate_block(b):
            first = pl.multiple_of(b * span, span)
            sum_block = running[pl.ds(first, span), :]
            terms = bc[b]
            for r in range(span):
                carried = jnp.exp(sum_block[r : r + 1] * rates) * entered[r % 2]
                reading[pl.ds(first + r, 1), :] += jnp.sum(
                    carried * terms[state_n : 2 * state_n, r : r + 1], axis=0, keepdims=True
                )
            drive = x_ref[pl.ds(first, span), :].astype(F32)
            gate = z_ref[pl.ds(first, span), :].astype(F32)
            value = (reading[pl.ds(first, span), :] + skip * drive) * (gate / (1.0 + jnp.exp(-gate)))
            gated[pl.ds(first, span), :] = value.astype(BF16)

        loop(0, blocks, gate_block)

    with jax.named_scope("project"):
        loop(0, nz, lambda i: sibling_copy(2 * i + 1 - core).wait_recv())

        def multiply(b):
            at = pl.multiple_of(b * columns, columns)
            out = jnp.dot(gated[...], wf[b], preferred_element_type=F32).astype(BF16)
            product[:, :, :, pl.ds(at, columns)] = out.reshape(ny, nx, own, columns)

        def row_copy(o):
            to = lax.rem(ex + o, nx)
            return remote(
                product.at[:, to, :, low], row_in.at[o - 1], a_send.at[0, o - 1], a_recv.at[0, o - 1],
                {"expert": ey * nx + to},
            )

        def col_copy(o):
            to = lax.rem(ey + o, ny)
            return remote(
                product.at[to, :, :, high], col_in.at[o - 1], b_send.at[0, o - 1], b_recv.at[0, o - 1],
                {"expert": to * nx + ex},
            )

        def row_pass(o):
            to = lax.rem(ey + o, ny)
            return remote(
                row_sum.at[to], row_last.at[o - 1], a_send.at[1, o - 1], a_recv.at[1, o - 1],
                {"expert": to * nx + ex},
            )

        def col_pass(o):
            to = lax.rem(ex + o, nx)
            return remote(
                col_sum.at[to], col_last.at[o - 1], b_send.at[1, o - 1], b_recv.at[1, o - 1],
                {"expert": ey * nx + to},
            )

        loop(0, ns // 2, multiply)
        loop(1, nx, lambda o: row_copy(o).start())
        loop(ns // 2, ns, multiply)
        loop(1, ny, lambda o: col_copy(o).start())
        loop(1, nx, lambda o: row_copy(o).wait_recv())

        def add_row(i):
            acc = product[i, ex, :, low].astype(F32)
            for o in range(nx - 1):
                acc = acc + row_in[o, i].astype(F32)
            row_sum[i] = acc.astype(BF16)

        loop(0, ny, add_row)
        loop(1, ny, lambda o: row_pass(o).start())
        loop(1, ny, lambda o: col_copy(o).wait_recv())

        def add_col(i):
            acc = product[ey, i, :, high].astype(F32)
            for o in range(ny - 1):
                acc = acc + col_in[o, i].astype(F32)
            col_sum[i] = acc.astype(BF16)

        loop(0, nx, add_col)
        loop(1, nx, lambda o: col_pass(o).start())
        loop(1, ny, lambda o: row_pass(o).wait_recv())
        acc = hid_ref[:, low].astype(F32) + row_sum[ey].astype(F32)
        for o in range(ny - 1):
            acc = acc + row_last[o].astype(F32)
        wide[:, low] = acc.astype(BF16).astype(F32)
        loop(1, nx, lambda o: col_pass(o).wait_recv())
        acc = hid_ref[:, high].astype(F32) + col_sum[ex].astype(F32)
        for o in range(nx - 1):
            acc = acc + col_last[o].astype(F32)
        wide[:, high] = acc.astype(BF16).astype(F32)

    def spread(value_of, target):
        for j in range(pieces):
            flat[pl.ds(j, count, stride=pieces), :] = value_of(j)
        target[...] = flat[...].astype(BF16).reshape(target.shape)

    def gather_pieces(source, target):
        flat[...] = source[...].astype(F32).reshape(flat.shape)
        for j in range(pieces):
            target[:, j * 128 : (j + 1) * 128] = flat[pl.ds(j, count, stride=pieces), :].astype(BF16)

    with jax.named_scope("route"):
        mixed = wide[...]
        mean = jnp.mean(mixed * mixed, axis=-1, keepdims=True)
        normed = (mixed * lax.rsqrt(mean + EPS) * gain_ref[...]).astype(BF16)
        spread(
            lambda j: jnp.dot(
                place_ref[...], normed[:, j * 128 : (j + 1) * 128], preferred_element_type=F32
            ),
            packed_out,
        )

        def send_rows(o):
            to = lax.rem(expert + o, ne)
            return remote(
                packed_out.at[to], packed_in.at[expert], d_send.at[o - 1], d_recv.at[o - 1], {"expert": to}
            )

        loop(1, ne, lambda o: send_rows(o).start())
        packed_in[expert] = packed_out[expert]
        logits = lax.dot_general(
            normed, router_ref[...], (((1,), (1,)), ((), ())), preferred_element_type=F32
        )
        scores = []
        for k in range(pick_ref.shape[0]):
            picked = jnp.sum(pick_ref[k] * logits, axis=-1, keepdims=True)
            scores.append(1.0 / (1.0 + jnp.exp(-picked)))
        all_scores = sum(scores)
        combine_w[...] = sum((score / all_scores) * put_ref[k] for k, score in enumerate(scores))
        loop(1, ne, lambda o: send_rows(o).wait_recv())
        gather_pieces(packed_in, held.at[0])

    def gather_copy(stage, forward):
        way = 0 if forward else 1
        source = held.at[2 * (stage - 1) + (0 if forward or stage == 1 else 1)]
        if stage < hops:
            target = held.at[2 * stage + way]
        else:
            picked = low if forward else high
            source, target = source.at[:, picked], held.at[1, :, picked]
        return remote(
            source, target, g_send.at[way, stage - 1], g_recv.at[way, stage - 1], {"seq": right if forward else left}
        )

    def return_copy(stage, forward):
        way = 0 if forward else 1
        buffer = from_left if forward else from_right
        distance = hops - stage + 1
        if stage == 1:
            picked = low if forward else high
            source, target = parts.at[1, :, picked], buffer.at[0, :, picked]
        else:
            source, target = parts.at[2 * distance + (1 if forward else 0)], buffer.at[stage - 1]
        return remote(
            source, target, r_send.at[way, stage - 1], r_recv.at[way, stage - 1], {"seq": right if forward else left}
        )

    def compute(pair):
        rows = held[2 * pair : 2 * pair + 2].reshape(2 * count, width)
        across = (((1,), (1,)), ((), ()))
        gate = lax.dot_general(rows, gate_w[...], across, preferred_element_type=F32)
        up = lax.dot_general(rows, up_w[...], across, preferred_element_type=F32)
        hidden[...] = (gate / (1.0 + jnp.exp(-gate)) * up).astype(BF16)
        step = min(width, 512)

        def down(b):
            at = pl.multiple_of(b * step, step)
            out = jnp.dot(hidden[...], down_w[:, pl.ds(at, step)], preferred_element_type=F32)
            parts[2 * pair : 2 * pair + 2, :, pl.ds(at, step)] = out.astype(BF16).reshape(2, count, step)

        loop(0, width // step, down)

    with jax.named_scope("experts"):
        gather_copy(1, True).start()
        gather_copy(1, False).start()
        for copy in loads:
            copy.wait()
        for copy in pairs:
            copy.wait_recv()
        for stage in range(1, hops + 1):
            gather_copy(stage, True).wait_recv()
            gather_copy(stage, False).wait_recv()
            if stage < hops:
                gather_copy(stage + 1, True).start()
                gather_copy(stage + 1, False).start()
            compute(stage if stage < hops else 0)

    with jax.named_scope("combine"):
        return_copy(1, True).start()
        return_copy(1, False).start()
        for stage in range(2, hops + 1):
            distance = hops - stage + 1
            for forward, buffer in ((True, from_left), (False, from_right)):
                return_copy(stage - 1, forward).wait_recv()
                slot = 2 * distance + (1 if forward else 0)
                picked = pl.ds(0, width) if stage > 2 else low if forward else high
                parts[slot, :, picked] = (
                    parts[slot, :, picked].astype(F32) + buffer[stage - 2, :, picked].astype(F32)
                ).astype(BF16)
                return_copy(stage, forward).start()
        return_copy(hops, True).wait_recv()
        return_copy(hops, False).wait_recv()

    with jax.named_scope("home"):

        def summed_piece(j):
            at = pl.ds(j * 128, 128)
            value = parts[0, :, at].astype(F32)
            if hops > 1 or j < pieces // 2:
                value = value + from_left[hops - 1, :, at].astype(F32)
            if hops > 1 or j >= pieces // 2:
                value = value + from_right[hops - 1, :, at].astype(F32)
            return value

        spread(summed_piece, back_out)

        def send_back(o):
            to = lax.rem(expert + o, ne)
            return remote(
                back_out.at[to], back_in.at[expert], e_send.at[o - 1], e_recv.at[o - 1], {"expert": to}
            )

        loop(1, ne, lambda o: send_back(o).start())
        back_in[expert] = back_out[expert]
        loop(1, ne, lambda o: send_back(o).wait_recv())
        gather_pieces(back_in, returned)
        weights_high = combine_w[...].astype(BF16)
        weights_low = (combine_w[...] - weights_high.astype(F32)).astype(BF16)
        routed = jnp.dot(weights_high, returned[...], preferred_element_type=F32) + jnp.dot(
            weights_low, returned[...], preferred_element_type=F32
        )
        out_ref[...] = (wide[...] + routed).astype(BF16)

    with jax.named_scope("finish"):

        def sent_peers(o):
            part_copy(o).wait_send()
            proj_copy(o).wait_send()
            send_rows(o).wait_send()
            send_back(o).wait_send()

        loop(1, ne, sent_peers)

        def sent_rows(o):
            row_copy(o).wait_send()
            col_pass(o).wait_send()

        def sent_cols(o):
            col_copy(o).wait_send()
            row_pass(o).wait_send()

        loop(1, nx, sent_rows)
        loop(1, ny, sent_cols)
        loop(plane + 1, nz, lambda to: state_copy(to, plane).wait_send())
        half_copy.wait_send()
        enter_copy.wait_send()
        for stage in range(1, hops + 1):
            ring_copy(stage, True).wait_send()
            for forward in (True, False):
                gather_copy(stage, forward).wait_send()
                return_copy(stage, forward).wait_send()
        for stage in range(1, back + 1):
            ring_copy(stage, False).wait_send()
        loop(0, nz, lambda i: sibling_copy(2 * i + core).wait_send())
        for copy in pairs:
            copy.wait_send()


def layer_call(
    ns, ne, cap, x, z, xp, dtw, dtb, rates, skip, w, hid, gain, router, place, pick, put, wg, wu, wd
):
    tokens, channels = x.shape
    own, width = hid.shape
    state_n = rates.shape[0]
    lanes = -(-xp.shape[0] // 128) * 128
    nz = ns // 2
    hops = nz // 2
    ny = 4 if ne == 16 else 2
    nx = ne // ny
    half = width // 2
    units = wg.shape[0]
    count = ne * cap
    pieces = width // 128
    dma = pltpu.SemaphoreType.DMA
    vmem = pltpu.VMEM
    return pl.pallas_call(
        functools.partial(layer_kernel, ns, ne, cap),
        out_shape=jax.ShapeDtypeStruct((own, width), BF16),
        in_specs=[VMEM] * 14 + [HBM] * 3,
        out_specs=VMEM,
        scratch_shapes=[
            vmem((ne, own, lanes), BF16),
            vmem((ne - 1, own, lanes), BF16),
            vmem((own, lanes), BF16),
            vmem((ne, own, lanes), BF16),
            vmem((tokens, channels), F32),
            vmem((tokens, channels), F32),
            vmem((tokens, channels), F32),
            vmem((tokens // (2 * BLOCK), 2 * state_n, 128), F32),
            vmem((2 * state_n + 8, channels), F32),
            vmem((2 * state_n + 8, channels // 2), F32),
            vmem((2 * state_n + 8, channels // 2), F32),
            vmem((nz, 2 * state_n + 8, channels // 2), F32),
            vmem((2 * state_n, channels), F32),
            vmem((tokens, channels), BF16),
            vmem((ns,) + w.shape, BF16),
            vmem((ny, nx, own, width), BF16),
            vmem((nx - 1, ny, own, half), BF16),
            vmem((ny, own, half), BF16),
            vmem((ny - 1, own, half), BF16),
            vmem((ny - 1, nx, own, half), BF16),
            vmem((nx, own, half), BF16),
            vmem((nx - 1, own, half), BF16),
            vmem((own, width), F32),
            vmem((own, count), F32),
            vmem((count * pieces, 128), F32),
            vmem((ne, cap * pieces, 128), BF16),
            vmem((ne, cap * pieces, 128), BF16),
            vmem((ne, cap * pieces, 128), BF16),
            vmem((ne, cap * pieces, 128), BF16),
            vmem((count, width), BF16),
            vmem((nz, count, width), BF16),
            vmem((nz, count, width), BF16),
            vmem((hops, count, width), BF16),
            vmem((hops, count, width), BF16),
            vmem((2 * units, width), BF16),
            vmem((2 * units, width), BF16),
            vmem((2 * units, width), BF16),
            vmem((2 * count, 2 * units), BF16),
            dma((3,)),
            dma((3,)), dma((3,)),
            dma((ne - 1,)), dma((ne - 1,)),
            dma((ne - 1,)), dma((ne - 1,)),
            dma((2,)), dma((2,)),
            dma((nz,)), dma((nz,)),
            dma((2, hops)), dma((2, hops)),
            dma((nz,)), dma((nz,)),
            dma((2, nx + ny)), dma((2, nx + ny)),
            dma((2, nx + ny)), dma((2, nx + ny)),
            dma((ne - 1,)), dma((ne - 1,)),
            dma((ne - 1,)), dma((ne - 1,)),
            dma((2, hops)), dma((2, hops)),
            dma((2, hops)), dma((2, hops)),
        ],
        compiler_params=pltpu.CompilerParams(
            collective_id=0, has_side_effects=True, vmem_limit_bytes=58 * 1024 * 1024
        ),
    )(x, z, xp, dtw, dtb, rates, skip, w, hid, gain, router, place, pick, put, wg, wu, wd)


def body(
    hidden_in,
    mamba_x,
    mamba_z,
    x_proj,
    dt_weight,
    dt_bias,
    state_rates,
    skip_gain,
    out_weight,
    norm_gain,
    router_weight,
    expert_ids,
    w_gate,
    w_up,
    w_down,
):
    ns, ne = lax.axis_size("seq"), lax.axis_size("expert")
    slice_len, docs, channels = mamba_x.shape
    model_width = hidden_in.shape[2]
    token_rows = hidden_in.shape[0] * docs
    experts = router_weight.shape[1]
    top_count = expert_ids.shape[2]
    capacity = max(2, min(token_rows, token_rows * top_count * 5 // (2 * experts)))
    chosen_ids = expert_ids.reshape(token_rows, top_count)
    expert_range = jnp.arange(experts, dtype=jnp.int32)
    flat_ids = chosen_ids.reshape(-1)
    marks = (flat_ids[:, None] == expert_range[None, :]).astype(jnp.int32)
    slots = jnp.sum((jnp.cumsum(marks, axis=0) - 1) * marks, axis=1)
    targets = (flat_ids * capacity + slots).reshape(token_rows, top_count)
    places = jnp.arange(experts * capacity, dtype=jnp.int32)
    place = jnp.any(places[:, None, None] == targets[None], axis=2).astype(jnp.bfloat16)
    pick = (chosen_ids.T[:, :, None] == expert_range).astype(jnp.float32)
    put = (targets.T[:, :, None] == places).astype(jnp.float32)
    result = layer_call(
        ns,
        ne,
        capacity,
        mamba_x.reshape(slice_len * docs, channels),
        mamba_z.reshape(slice_len * docs, channels),
        x_proj.T,
        dt_weight,
        dt_bias[None],
        state_rates.T,
        skip_gain[None],
        out_weight,
        hidden_in.reshape(token_rows, model_width),
        norm_gain[None],
        router_weight.T,
        place,
        pick,
        put,
        w_gate[0].T,
        w_up[0].T,
        w_down[0].T,
    )
    return result.reshape(hidden_in.shape)


def solution(mesh):
    placed = (
        P(("seq", "expert"), None, None),
        P("seq", None, "expert"),
        P("seq", None, "expert"),
        P("expert", None),
        P(None, "expert"),
        P("expert"),
        P("expert", None),
        P("expert"),
        P("expert", "seq"),
        P(),
        P(),
        P(("seq", "expert"), None, None),
        P("expert", None, "seq"),
        P("expert", None, "seq"),
        P("expert", None, "seq"),
    )
    return jax.shard_map(
        body,
        mesh=mesh,
        in_specs=placed,
        out_specs=P(("seq", "expert"), None, None),
        check_vma=False,
    )
```

time: 269 us -> 211 us (0.78)
  waiting for transfers between devices: 27.7 us -> 0 us
  local copies, waits for them, and re-layouts: 32.7 us -> 9.06 us
  starting transfers between devices: 17 us -> 0 us
  Pallas kernels: 189 us -> 199 us
    all_to_all x2 -> x0, waiting for transfers between devices: 27.7 us -> none  [the longest x1 14.9 us: body(): lax.all_to_all(outgoing_rows, 'expert', split_axis=0, concat_axis=0, tile...]
    unnamed x24 -> x2, local copies, waits for them, and re-layouts: 23.4 us -> 1.53 us
    all_to_all x2 -> x0, starting transfers between devices: 17 us -> none  [the longest x1 11.2 us: body(): lax.all_to_all(outgoing_rows, 'expert', split_axis=0, concat_axis=0, tile...]
    pallas_call x2 -> x1, Pallas kernels: 189 us -> 199 us  [layer_call(): pl.pallas_call(functools.partial(layer_kernel, ns, ne, cap), out_shape=ja...]
    reshape x5 -> x0, local copies, waits for them, and re-layouts: 5.22 us -> none  [the longest x1 2.34 us: body(): expert_back = summed.reshape(arrived.shape)]
  transfers between devices with their start and end apart: 2 -> 0, of which waited for: 2 -> 0; matrix products, arithmetic and copies ran while one was open for 0% -> 0% of each run, Pallas kernels for 0% -> 0%
where the time goes in v2:
time: 211 us; the launch traced here: 210 us
  Pallas kernels  199 us (94%)
  local copies, waits for them, and re-layouts  9.06 us (4%)
    pallas_call x1, Pallas kernels, layer_call(): pl.pallas_call(functools.partial(layer_kernel, ns, ne, cap), out_shape=ja...  199 us

profile of v2, /device:TPU:2, one launch (start us, length us, event | category | flops | bytes accessed | tf_op | source)
XLA Modules:
  0.0 210.3 jit_solution(3013610934781534125)
XLA Ops:
  0.0 0.8 copy.29
  0.8 0.1 eq.27
  0.9 0.8 copy.28
  1.6 0.1 reshape_reshape.3
  1.7 0.7 fusion.2.pick_ref
  2.4 0.1 fusion
  2.5 0.1 reduce_window_sum.11
  2.5 0.2 select_reduce_fusion
  2.7 0.1 reduce_sum.12
  2.8 0.1 copy.30
  2.9 0.1 fusion.1
  3.0 0.7 copy.31.place_ref
  3.7 0.7 fusion.3.put_ref
  4.3 1.6 reshape.31.hid_ref
  6.0 1.6 reshape.29.x_ref
  7.6 1.6 reshape.30.z_ref
  9.2 199.4 %shard_map.145 = bf16[16,4096]{1,0:T(8,128)(2,1)} custom-call(bf16[256,256]{1,0:T(8,128)(2,1)} %reshape.29.x_ref, bf16[256,256]{1,0:T(8,128)(2,1)} %reshape.30.z_ref, bf16[288,256]{1,0:T(8,128)(2,1)} %bitcast.22, bf16[256,256]{1,0:T(8,128)(2,1)} %dtw_ref.1, f32[1,256]{1,0:T(1,128)} %bitcast.28, f32[16,256]{1,0:T(8,128)} %bitcast.24, f32[1,256]{1,0:T(1,128)} %bitcast.29, ...), custom_call_target="tpu_custom_call" | custom-call | tf_op jit(solution)/shard_map/pallas_call | solution.py:537
  208.6 1.7 reshape.32
  (2 shorter events, 0.0 us)

commit v3 on v2

--- a/solution.py
+++ b/solution.py
@@ -48,9 +48,10 @@
 
 def layer_kernel(
     ns, ne, cap,
-    x_ref, z_ref, xp_ref, dtw_ref, dtb_ref, rates_ref, skip_ref, w_ref, hid_ref,
-    gain_ref, router_ref, place_ref, pick_ref, put_ref, wg_ref, wu_ref, wd_ref,
+    x_in, z_in, xp_ref, dtw_ref, dtb_ref, rates_ref, skip_ref, w_ref, hid_in,
+    gain_ref, router_ref, ids_ref, wg_ref, wu_ref, wd_ref,
     out_ref,
+    x_ref, z_ref, hid_ref, place_ref, pick_ref, put_ref,
     part, part_in, part_sum, proj, sizes, running, reading, bc,
     state, state_sib, state_chip, state_in, incoming, gated, wf,
     product, row_in, row_sum, row_last, col_in, col_sum, col_last,
@@ -112,6 +113,33 @@
         if stage <= back:
             ring_copy(stage, False).start()
 
+    def choose():
+        docs, picks, positions = ids_ref.shape
+
+        def grid(shape, axis):
+            return lax.broadcasted_iota(jnp.int32, shape, axis)
+
+        chosen, marks = [], []
+        for k in range(picks):
+            found = jnp.zeros((own, 1), F32)
+            for d in range(docs):
+                here = grid((own, positions), 0) == grid((own, positions), 1) * docs + d
+                row = ids_ref[d, k : k + 1, :].astype(F32)
+                found = found + jnp.sum(jnp.where(here, row, 0.0), axis=1, keepdims=True)
+            chosen.append(found)
+            marks.append((grid((own, ne), 1).astype(F32) == found).astype(F32))
+            pick_ref[k] = marks[k]
+        before = (grid((own, own), 0) > grid((own, own), 1)).astype(BF16)
+        taken = jnp.dot(before, sum(marks).astype(BF16), preferred_element_type=F32)
+        for k in range(picks):
+            slot = jnp.sum(marks[k] * taken, axis=1, keepdims=True)
+            target = chosen[k] * cap + slot
+            put_ref[k] = (grid((own, count), 1).astype(F32) == target).astype(F32)
+        eye = (grid((own, own), 0) == grid((own, own), 1)).astype(BF16)
+        place_ref[...] = lax.dot_general(
+            (put_ref[0] + put_ref[1]).astype(BF16), eye, (((0,), (0,)), ((), ())), preferred_element_type=F32
+        ).astype(BF16)
+
     with jax.named_scope("greet"):
         weights = ((wg_ref, gate_w), (wu_ref, up_w), (wd_ref, down_w))
         loads = [
@@ -121,6 +149,7 @@
         for copy in loads:
             copy.start()
         wf[seq] = w_ref[...]
+        x_ref[...] = x_in[...].reshape(tokens, channels)
         greet(ns, ne, seq, expert)
         ring_stage(1)
         sibling_copy(seq).start()
@@ -142,6 +171,9 @@
             for i, (src, dst) in enumerate(weights)
         ]
 
+        z_ref[...] = z_in[...].reshape(tokens, channels)
+        hid_ref[...] = hid_in[...].reshape(own, width)
+
         def add_part(o, acc):
             part_copy(o).wait_recv()
             return acc + part_in[o - 1].astype(F32)
@@ -156,6 +188,7 @@
 
         loop(1, ne, lambda o: proj_copy(o).start())
         ring_stage(2)
+        choose()
         loop(1, ne, lambda o: proj_copy(o).wait_recv())
 
     with jax.named_scope("sizes"):
@@ -227,8 +260,6 @@
             return remote(state_chip, state_in.at[source], s_send.at[to], s_recv.at[source], {"seq": to * 2 + core})
 
         loop(plane + 1, nz, lambda to: state_copy(to, plane).start())
-        for copy in pairs:
-            copy.start()
 
         def horner(source, carry):
             state_copy(plane, source).wait_recv()
@@ -247,6 +278,8 @@
         enter_copy.start()
         for stage in range(4, hops + 2):
             ring_stage(stage)
+        for copy in pairs:
+            copy.start()
         enter_copy.wait_recv()
 
     with jax.named_scope("gate"):
@@ -340,35 +373,39 @@
             acc = acc + col_last[o].astype(F32)
         wide[:, high] = acc.astype(BF16).astype(F32)
 
-    def spread(value_of, target):
-        for j in range(pieces):
-            flat[pl.ds(j, count, stride=pieces), :] = value_of(j)
-        target[...] = flat[...].astype(BF16).reshape(target.shape)
-
-    def gather_pieces(source, target):
-        flat[...] = source[...].astype(F32).reshape(flat.shape)
-        for j in range(pieces):
-            target[:, j * 128 : (j + 1) * 128] = flat[pl.ds(j, count, stride=pieces), :].astype(BF16)
+    sides = (low, high)
+    each = pieces // 2
+
+    def spread(value_of, target, h):
+        for j in range(each):
+            flat[pl.ds(j, count, stride=each), :] = value_of(h * each + j)
+        target[h] = flat[...].astype(BF16).reshape(target.shape[1:])
+
+    def gather_pieces(source, target, h):
+        flat[...] = source[h].astype(F32).reshape(flat.shape)
+        for j in range(each):
+            at = h * half + j * 128
+            target[:, at : at + 128] = flat[pl.ds(j, count, stride=each), :].astype(BF16)
 
     with jax.named_scope("route"):
         mixed = wide[...]
         mean = jnp.mean(mixed * mixed, axis=-1, keepdims=True)
         normed = (mixed * lax.rsqrt(mean + EPS) * gain_ref[...]).astype(BF16)
-        spread(
-            lambda j: jnp.dot(
-                place_ref[...], normed[:, j * 128 : (j + 1) * 128], preferred_element_type=F32
-            ),
-            packed_out,
-        )
-
-        def send_rows(o):
+
+        def send_rows(o, h):
             to = lax.rem(expert + o, ne)
             return remote(
-                packed_out.at[to], packed_in.at[expert], d_send.at[o - 1], d_recv.at[o - 1], {"expert": to}
+                packed_out.at[h, to], packed_in.at[h, expert], d_send.at[h, o - 1], d_recv.at[h, o - 1],
+                {"expert": to},
             )
 
-        loop(1, ne, lambda o: send_rows(o).start())
-        packed_in[expert] = packed_out[expert]
+        def placed(j):
+            return jnp.dot(place_ref[...], normed[:, j * 128 : (j + 1) * 128], preferred_element_type=F32)
+
+        for h in range(2):
+            spread(placed, packed_out, h)
+            loop(1, ne, lambda o: send_rows(o, h).start())
+            packed_in[h, expert] = packed_out[h, expert]
         logits = lax.dot_general(
             normed, router_ref[...], (((1,), (1,)), ((), ())), preferred_element_type=F32
         )
@@ -378,33 +415,29 @@
             scores.append(1.0 / (1.0 + jnp.exp(-picked)))
         all_scores = sum(scores)
         combine_w[...] = sum((score / all_scores) * put_ref[k] for k, score in enumerate(scores))
-        loop(1, ne, lambda o: send_rows(o).wait_recv())
-        gather_pieces(packed_in, held.at[0])
-
-    def gather_copy(stage, forward):
+
+    def gather_copy(stage, forward, h):
         way = 0 if forward else 1
-        source = held.at[2 * (stage - 1) + (0 if forward or stage == 1 else 1)]
-        if stage < hops:
-            target = held.at[2 * stage + way]
-        else:
-            picked = low if forward else high
-            source, target = source.at[:, picked], held.at[1, :, picked]
+        source = held.at[2 * (stage - 1) + (0 if forward or stage == 1 else 1), :, sides[h]]
+        target = held.at[2 * stage + way if stage < hops else 1, :, sides[h]]
         return remote(
-            source, target, g_send.at[way, stage - 1], g_recv.at[way, stage - 1], {"seq": right if forward else left}
-        )
-
-    def return_copy(stage, forward):
+            source, target, g_send.at[way, h, stage - 1], g_recv.at[way, h, stage - 1],
+            {"seq": right if forward else left},
+        )
+
+    def return_copy(stage, forward, h):
         way = 0 if forward else 1
         buffer = from_left if forward else from_right
-        distance = hops - stage + 1
-        if stage == 1:
-            picked = low if forward else high
-            source, target = parts.at[1, :, picked], buffer.at[0, :, picked]
-        else:
-            source, target = parts.at[2 * distance + (1 if forward else 0)], buffer.at[stage - 1]
+        slot = 2 * (hops - stage + 1) + way_of(forward) if stage > 1 else 1
         return remote(
-            source, target, r_send.at[way, stage - 1], r_recv.at[way, stage - 1], {"seq": right if forward else left}
-        )
+            parts.at[slot, :, sides[h]], buffer.at[stage - 1, :, sides[h]],
+            r_send.at[way, h, stage - 1], r_recv.at[way, h, stage - 1], {"seq": right if forward else left},
+        )
+
+    def way_of(forward):
+        return 1 if forward else 0
+
+    ways = ((True, 0, 1), (False, 1, 0))
 
     def compute(pair):
         rows = held[2 * pair : 2 * pair + 2].reshape(2 * count, width)
@@ -422,73 +455,98 @@
         loop(0, width // step, down)
 
     with jax.named_scope("experts"):
-        gather_copy(1, True).start()
-        gather_copy(1, False).start()
+        for h in range(2):
+            loop(1, ne, lambda o: send_rows(o, h).wait_recv())
+            gather_pieces(packed_in, held.at[0], h)
+            for forward, early, late in ways:
+                if hops > 1 or h == early:
+                    gather_copy(1, forward, h).start()
         for copy in loads:
             copy.wait()
         for copy in pairs:
             copy.wait_recv()
-        for stage in range(1, hops + 1):
-            gather_copy(stage, True).wait_recv()
-            gather_copy(stage, False).wait_recv()
-            if stage < hops:
-                gather_copy(stage + 1, True).start()
-                gather_copy(stage + 1, False).start()
-            compute(stage if stage < hops else 0)
+        for stage in range(1, hops - 1):
+            last = stage == hops - 2
+            for h in range(2):
+                for forward, early, late in ways:
+                    gather_copy(stage, forward, h).wait_recv()
+                    if not last or h == early:
+                        gather_copy(stage + 1, forward, h).start()
+            compute(stage)
+        for forward, early, late in ways:
+            if hops > 1:
+                gather_copy(hops - 1, forward, early).wait_recv()
+                gather_copy(hops, forward, early).start()
+                if hops > 2:
+                    gather_copy(hops - 1, forward, late).start()
+        for forward, early, late in ways:
+            gather_copy(hops, forward, early).wait_recv()
+        compute(0)
+        for forward, early, late in ways:
+            return_copy(1, forward, early).start()
+        if hops > 1:
+            for forward, early, late in ways:
+                gather_copy(hops - 1, forward, late).wait_recv()
+            compute(hops - 1)
 
     with jax.named_scope("combine"):
-        return_copy(1, True).start()
-        return_copy(1, False).start()
         for stage in range(2, hops + 1):
-            distance = hops - stage + 1
-            for forward, buffer in ((True, from_left), (False, from_right)):
-                return_copy(stage - 1, forward).wait_recv()
-                slot = 2 * distance + (1 if forward else 0)
-                picked = pl.ds(0, width) if stage > 2 else low if forward else high
-                parts[slot, :, picked] = (
-                    parts[slot, :, picked].astype(F32) + buffer[stage - 2, :, picked].astype(F32)
-                ).astype(BF16)
-                return_copy(stage, forward).start()
-        return_copy(hops, True).wait_recv()
-        return_copy(hops, False).wait_recv()
+            for h in range(2):
+                for forward, early, late in ways:
+                    if stage > 2 or h == early:
+                        return_copy(stage - 1, forward, h).wait_recv()
+                        buffer = from_left if forward else from_right
+                        slot = 2 * (hops - stage + 1) + way_of(forward)
+                        parts[slot, :, sides[h]] = (
+                            parts[slot, :, sides[h]].astype(F32) + buffer[stage - 2, :, sides[h]].astype(F32)
+                        ).astype(BF16)
+                    return_copy(stage, forward, h).start()
 
     with jax.named_scope("home"):
 
         def summed_piece(j):
             at = pl.ds(j * 128, 128)
             value = parts[0, :, at].astype(F32)
-            if hops > 1 or j < pieces // 2:
-                value = value + from_left[hops - 1, :, at].astype(F32)
-            if hops > 1 or j >= pieces // 2:
-                value = value + from_right[hops - 1, :, at].astype(F32)
+            for forward, early, late in ways:
+                if hops > 1 or j // each == early:
+                    buffer = from_left if forward else from_right
+                    value = value + buffer[hops - 1, :, at].astype(F32)
             return value
 
-        spread(summed_piece, back_out)
-
-        def send_back(o):
+        def send_back(o, h):
             to = lax.rem(expert + o, ne)
             return remote(
-                back_out.at[to], back_in.at[expert], e_send.at[o - 1], e_recv.at[o - 1], {"expert": to}
+                back_out.at[h, to], back_in.at[h, expert], e_send.at[h, o - 1], e_recv.at[h, o - 1],
+                {"expert": to},
             )
 
-        loop(1, ne, lambda o: send_back(o).start())
-        back_in[expert] = back_out[expert]
-        loop(1, ne, lambda o: send_back(o).wait_recv())
-        gather_pieces(back_in, returned)
+        for h in range(2):
+            for forward, early, late in ways:
+                if hops > 1 or h == early:
+                    return_copy(hops, forward, h).wait_recv()
+            spread(summed_piece, back_out, h)
+            loop(1, ne, lambda o: send_back(o, h).start())
+            back_in[h, expert] = back_out[h, expert]
         weights_high = combine_w[...].astype(BF16)
         weights_low = (combine_w[...] - weights_high.astype(F32)).astype(BF16)
-        routed = jnp.dot(weights_high, returned[...], preferred_element_type=F32) + jnp.dot(
-            weights_low, returned[...], preferred_element_type=F32
-        )
-        out_ref[...] = (wide[...] + routed).astype(BF16)
+        for h in range(2):
+            loop(1, ne, lambda o: send_back(o, h).wait_recv())
+            gather_pieces(back_in, returned, h)
+            values = returned[:, sides[h]]
+            routed = jnp.dot(weights_high, values, preferred_element_type=F32) + jnp.dot(
+                weights_low, values, preferred_element_type=F32
+            )
+            mixed = (wide[:, sides[h]] + routed).astype(BF16)
+            out_ref[:, :, sides[h]] = mixed.reshape(out_ref.shape[:2] + (half,))
 
     with jax.named_scope("finish"):
 
         def sent_peers(o):
             part_copy(o).wait_send()
             proj_copy(o).wait_send()
-            send_rows(o).wait_send()
-            send_back(o).wait_send()
+            for h in range(2):
+                send_rows(o, h).wait_send()
+                send_back(o, h).wait_send()
 
         loop(1, ne, sent_peers)
 
@@ -507,9 +565,12 @@
         enter_copy.wait_send()
         for stage in range(1, hops + 1):
             ring_copy(stage, True).wait_send()
-            for forward in (True, False):
-                gather_copy(stage, forward).wait_send()
-                return_copy(stage, forward).wait_send()
+            for forward, early, late in ways:
+                for h in range(2):
+                    if stage < hops or h == early:
+                        gather_copy(stage, forward, h).wait_send()
+                    if stage > 1 or h == early:
+                        return_copy(stage, forward, h).wait_send()
         for stage in range(1, back + 1):
             ring_copy(stage, False).wait_send()
         loop(0, nz, lambda i: sibling_copy(2 * i + core).wait_send())
@@ -518,10 +579,11 @@
 
 
 def layer_call(
-    ns, ne, cap, x, z, xp, dtw, dtb, rates, skip, w, hid, gain, router, place, pick, put, wg, wu, wd
+    ns, ne, cap, x, z, xp, dtw, dtb, rates, skip, w, hid, gain, router, ids, wg, wu, wd
 ):
-    tokens, channels = x.shape
-    own, width = hid.shape
+    tokens, channels = x.shape[0] * x.shape[1], x.shape[2]
+    own, width = hid.shape[0] * hid.shape[1], hid.shape[2]
+    picks = ids.shape[1]
     state_n = rates.shape[0]
     lanes = -(-xp.shape[0] // 128) * 128
     nz = ns // 2
@@ -536,10 +598,16 @@
     vmem = pltpu.VMEM
     return pl.pallas_call(
         functools.partial(layer_kernel, ns, ne, cap),
-        out_shape=jax.ShapeDtypeStruct((own, width), BF16),
-        in_specs=[VMEM] * 14 + [HBM] * 3,
+        out_shape=jax.ShapeDtypeStruct(hid.shape, BF16),
+        in_specs=[VMEM] * 12 + [HBM] * 3,
         out_specs=VMEM,
         scratch_shapes=[
+            vmem((tokens, channels), BF16),
+            vmem((tokens, channels), BF16),
+            vmem((own, width), BF16),
+            vmem((count, own), BF16),
+            vmem((picks, own, ne), F32),
+            vmem((picks, own, count), F32),
             vmem((ne, own, lanes), BF16),
             vmem((ne - 1, own, lanes), BF16),
             vmem((own, lanes), BF16),
@@ -564,11 +632,11 @@
             vmem((nx - 1, own, half), BF16),
             vmem((own, width), F32),
             vmem((own, count), F32),
-            vmem((count * pieces, 128), F32),
-            vmem((ne, cap * pieces, 128), BF16),
-            vmem((ne, cap * pieces, 128), BF16),
-            vmem((ne, cap * pieces, 128), BF16),
-            vmem((ne, cap * pieces, 128), BF16),
+            vmem((count * pieces // 2, 128), F32),
+            vmem((2, ne, cap * pieces // 2, 128), BF16),
+            vmem((2, ne, cap * pieces // 2, 128), BF16),
+            vmem((2, ne, cap * pieces // 2, 128), BF16),
+            vmem((2, ne, cap * pieces // 2, 128), BF16),
             vmem((count, width), BF16),
             vmem((nz, count, width), BF16),
             vmem((nz, count, width), BF16),
@@ -588,15 +656,15 @@
             dma((nz,)), dma((nz,)),
             dma((2, nx + ny)), dma((2, nx + ny)),
             dma((2, nx + ny)), dma((2, nx + ny)),
-            dma((ne - 1,)), dma((ne - 1,)),
-            dma((ne - 1,)), dma((ne - 1,)),
-            dma((2, hops)), dma((2, hops)),
-            dma((2, hops)), dma((2, hops)),
+            dma((2, ne - 1)), dma((2, ne - 1)),
+            dma((2, ne - 1)), dma((2, ne - 1)),
+            dma((2, 2, hops)), dma((2, 2, hops)),
+            dma((2, 2, hops)), dma((2, 2, hops)),
         ],
         compiler_params=pltpu.CompilerParams(
             collective_id=0, has_side_effects=True, vmem_limit_bytes=58 * 1024 * 1024
         ),
-    )(x, z, xp, dtw, dtb, rates, skip, w, hid, gain, router, place, pick, put, wg, wu, wd)
+    )(x, z, xp, dtw, dtb, rates, skip, w, hid, gain, router, ids, wg, wu, wd)
 
 
 def body(
@@ -617,45 +685,30 @@
     w_down,
 ):
     ns, ne = lax.axis_size("seq"), lax.axis_size("expert")
-    slice_len, docs, channels = mamba_x.shape
-    model_width = hidden_in.shape[2]
-    token_rows = hidden_in.shape[0] * docs
+    token_rows = hidden_in.shape[0] * hidden_in.shape[1]
     experts = router_weight.shape[1]
     top_count = expert_ids.shape[2]
     capacity = max(2, min(token_rows, token_rows * top_count * 5 // (2 * experts)))
-    chosen_ids = expert_ids.reshape(token_rows, top_count)
-    expert_range = jnp.arange(experts, dtype=jnp.int32)
-    flat_ids = chosen_ids.reshape(-1)
-    marks = (flat_ids[:, None] == expert_range[None, :]).astype(jnp.int32)
-    slots = jnp.sum((jnp.cumsum(marks, axis=0) - 1) * marks, axis=1)
-    targets = (flat_ids * capacity + slots).reshape(token_rows, top_count)
-    places = jnp.arange(experts * capacity, dtype=jnp.int32)
-    place = jnp.any(places[:, None, None] == targets[None], axis=2).astype(jnp.bfloat16)
-    pick = (chosen_ids.T[:, :, None] == expert_range).astype(jnp.float32)
-    put = (targets.T[:, :, None] == places).astype(jnp.float32)
-    result = layer_call(
+    return layer_call(
         ns,
         ne,
         capacity,
-        mamba_x.reshape(slice_len * docs, channels),
-        mamba_z.reshape(slice_len * docs, channels),
+        mamba_x,
+        mamba_z,
         x_proj.T,
         dt_weight,
         dt_bias[None],
         state_rates.T,
         skip_gain[None],
         out_weight,
-        hidden_in.reshape(token_rows, model_width),
+        hidden_in,
         norm_gain[None],
         router_weight.T,
-        place,
-        pick,
-        put,
+        jnp.transpose(expert_ids, (1, 2, 0)),
         w_gate[0].T,
         w_up[0].T,
         w_down[0].T,
     )
-    return result.reshape(hidden_in.shape)
 
 
 def solution(mesh):

time: 211 us -> 187 us (0.89)
  Pallas kernels: 199 us -> 185 us
  local copies, waits for them, and re-layouts: 9.06 us -> 1.65 us
    pallas_call x1, Pallas kernels: 199 us -> 185 us  [layer_call(): pl.pallas_call(functools.partial(layer_kernel, ns, ne, cap), out_shape=ja...]
    reshape x4 -> x0, local copies, waits for them, and re-layouts: 6.48 us -> none  [the longest x1 1.67 us: body(): return result.reshape(hidden_in.shape)]
where the time goes in v3:
time: 187 us
  Pallas kernels  185 us (99%)
    pallas_call x1, Pallas kernels, layer_call(): pl.pallas_call(functools.partial(layer_kernel, ns, ne, cap), out_shape=ja...  185 us

profile of v3, /device:TPU:2, one launch (start us, length us, event | category | flops | bytes accessed | tf_op | source)
XLA Modules:
  0.0 187.0 jit_solution(895048403905299428)
XLA Ops:
  0.0 185.4 %shard_map.145 = bf16[8,2,4096]{2,1,0:T(2,128)(2,1)} custom-call(bf16[128,2,256]{2,1,0:T(2,128)(2,1)} %x_in.1, bf16[128,2,256]{2,1,0:T(2,128)(2,1)} %z_in.1, bf16[288,256]{1,0:T(8,128)(2,1)} %bitcast.19, bf16[256,256]{1,0:T(8,128)(2,1)} %dtw_ref.1, f32[1,256]{1,0:T(1,128)} %bitcast.24, f32[16,256]{1,0:T(8,128)} %bitcast.21, f32[1,256]{1,0:T(1,128)} %bitcast.25, ...), custom_call_target="tpu_custom_call" | custom-call | tf_op jit(solution)/shard_map/pallas_call | solution.py:599
  185.4 1.7 copy.17

commit v4 on v3

--- a/solution.py
+++ b/solution.py
@@ -55,12 +55,14 @@
     part, part_in, part_sum, proj, sizes, running, reading, bc,
     state, state_sib, state_chip, state_in, incoming, gated, wf,
     product, row_in, row_sum, row_last, col_in, col_sum, col_last,
+    scale_out, scale_in, scale_held,
     wide, combine_w, flat, packed_out, packed_in, back_out, back_in, returned,
+    q_out, q_in, t_out, t_in, routed_high,
     held, parts, from_left, from_right, gate_w, up_w, down_w, hidden,
     load_sem, pair_send, pair_recv, p1_send, p1_recv, p2_send, p2_recv,
     h_send, h_recv, s_send, s_recv, ring_send, ring_recv, sib_send, sib_recv,
-    a_send, a_recv, b_send, b_recv, d_send, d_recv, e_send, e_recv,
-    g_send, g_recv, r_send, r_recv,
+    a_send, a_recv, b_send, b_recv, c_send, c_recv, z_send, z_recv, d_send, d_recv, e_send, e_recv,
+    g_send, g_recv, r_send, r_recv, q_send, q_recv, t_send, t_recv, k_send, k_recv,
 ):
     seq, expert = lax.axis_index("seq"), lax.axis_index("expert")
     nz = ns // 2
@@ -77,6 +79,10 @@
     own, width = hid_ref.shape
     half = width // 2
     low, high = pl.ds(0, half), pl.ds(half, half)
+
+    def quarter(i):
+        return pl.ds(i * (half // 2), half // 2)
+
     blocks = tokens // (2 * BLOCK)
     span = 2 * BLOCK
     columns = w_ref.shape[1]
@@ -113,12 +119,11 @@
         if stage <= back:
             ring_copy(stage, False).start()
 
+    def grid(shape, axis):
+        return lax.broadcasted_iota(jnp.int32, shape, axis)
+
     def choose():
         docs, picks, positions = ids_ref.shape
-
-        def grid(shape, axis):
-            return lax.broadcasted_iota(jnp.int32, shape, axis)
-
         chosen, marks = [], []
         for k in range(picks):
             found = jnp.zeros((own, 1), F32)
@@ -134,10 +139,10 @@
         for k in range(picks):
             slot = jnp.sum(marks[k] * taken, axis=1, keepdims=True)
             target = chosen[k] * cap + slot
-            put_ref[k] = (grid((own, count), 1).astype(F32) == target).astype(F32)
+            put_ref[k] = (grid(put_ref.shape[1:], 1).astype(F32) == target).astype(F32)
         eye = (grid((own, own), 0) == grid((own, own), 1)).astype(BF16)
         place_ref[...] = lax.dot_general(
-            (put_ref[0] + put_ref[1]).astype(BF16), eye, (((0,), (0,)), ((), ())), preferred_element_type=F32
+            sum(put_ref[k] for k in range(picks))[:, :count].astype(BF16), eye, (((0,), (0,)), ((), ())), preferred_element_type=F32
         ).astype(BF16)
 
     with jax.named_scope("greet"):
@@ -190,6 +195,7 @@
         ring_stage(2)
         choose()
         loop(1, ne, lambda o: proj_copy(o).wait_recv())
+        ring_stage(3)
 
     with jax.named_scope("sizes"):
         proj_all = proj[...].reshape(tokens, proj.shape[2])
@@ -238,7 +244,7 @@
         other = pl.ds(pl.multiple_of((1 - core) * side, side), side)
         half_copy = remote(state.at[:, other], state_sib, h_send.at[0], h_recv.at[0], sibling)
         half_copy.start()
-        ring_stage(3)
+        ring_stage(4)
         rates_mine = -rates_ref[:, mine]
 
         def through(message, d):
@@ -260,6 +266,9 @@
             return remote(state_chip, state_in.at[source], s_send.at[to], s_recv.at[source], {"seq": to * 2 + core})
 
         loop(plane + 1, nz, lambda to: state_copy(to, plane).start())
+        ring_stage(5)
+        for copy in pairs:
+            copy.start()
 
         def horner(source, carry):
             state_copy(plane, source).wait_recv()
@@ -276,10 +285,6 @@
             state_sib.at[pl.ds(0, 2 * state_n)], incoming.at[:, mine], h_send.at[1], h_recv.at[1], sibling
         )
         enter_copy.start()
-        for stage in range(4, hops + 2):
-            ring_stage(stage)
-        for copy in pairs:
-            copy.start()
         enter_copy.wait_recv()
 
     with jax.named_scope("gate"):
@@ -310,68 +315,78 @@
             out = jnp.dot(gated[...], wf[b], preferred_element_type=F32).astype(BF16)
             product[:, :, :, pl.ds(at, columns)] = out.reshape(ny, nx, own, columns)
 
-        def row_copy(o):
+        def row_copy(o, g):
             to = lax.rem(ex + o, nx)
             return remote(
-                product.at[:, to, :, low], row_in.at[o - 1], a_send.at[0, o - 1], a_recv.at[0, o - 1],
+                product.at[:, to, :, quarter(2 * g)], row_in.at[g, o - 1], a_send.at[g, o - 1], a_recv.at[g, o - 1],
                 {"expert": ey * nx + to},
             )
 
-        def col_copy(o):
+        def col_copy(o, g):
             to = lax.rem(ey + o, ny)
             return remote(
-                product.at[to, :, :, high], col_in.at[o - 1], b_send.at[0, o - 1], b_recv.at[0, o - 1],
+                product.at[to, :, :, quarter(2 * g + 1)], col_in.at[g, o - 1], b_send.at[g, o - 1], b_recv.at[g, o - 1],
                 {"expert": to * nx + ex},
             )
 
-        def row_pass(o):
+        def row_pass(o, g):
             to = lax.rem(ey + o, ny)
             return remote(
-                row_sum.at[to], row_last.at[o - 1], a_send.at[1, o - 1], a_recv.at[1, o - 1],
+                row_sum.at[g, to], row_last.at[g, o - 1], a_send.at[2 + g, o - 1], a_recv.at[2 + g, o - 1],
                 {"expert": to * nx + ex},
             )
 
-        def col_pass(o):
+        def col_pass(o, g):
             to = lax.rem(ex + o, nx)
             return remote(
-                col_sum.at[to], col_last.at[o - 1], b_send.at[1, o - 1], b_recv.at[1, o - 1],
+                col_sum.at[g, to], col_last.at[g, o - 1], b_send.at[2 + g, o - 1], b_recv.at[2 + g, o - 1],
                 {"expert": ey * nx + to},
             )
 
+        def start_group(g):
+            loop(1, nx, lambda o: row_copy(o, g).start())
+            loop(1, ny, lambda o: col_copy(o, g).start())
+
+        def pass_group(g):
+            loop(1, nx, lambda o: row_copy(o, g).wait_recv())
+
+            def add_row(i):
+                acc = product[i, ex, :, quarter(2 * g)].astype(F32)
+                for o in range(nx - 1):
+                    acc = acc + row_in[g, o, i].astype(F32)
+                row_sum[g, i] = acc.astype(BF16)
+
+            loop(0, ny, add_row)
+            loop(1, ny, lambda o: row_pass(o, g).start())
+            loop(1, ny, lambda o: col_copy(o, g).wait_recv())
+
+            def add_col(i):
+                acc = product[ey, i, :, quarter(2 * g + 1)].astype(F32)
+                for o in range(ny - 1):
+                    acc = acc + col_in[g, o, i].astype(F32)
+                col_sum[g, i] = acc.astype(BF16)
+
+            loop(0, nx, add_col)
+            loop(1, nx, lambda o: col_pass(o, g).start())
+
+        def finish_group(g):
+            loop(1, ny, lambda o: row_pass(o, g).wait_recv())
+            acc = hid_ref[:, quarter(2 * g)].astype(F32) + row_sum[g, ey].astype(F32)
+            for o in range(ny - 1):
+                acc = acc + row_last[g, o].astype(F32)
+            wide[:, quarter(2 * g)] = acc.astype(BF16).astype(F32)
+            loop(1, nx, lambda o: col_pass(o, g).wait_recv())
+            acc = hid_ref[:, quarter(2 * g + 1)].astype(F32) + col_sum[g, ex].astype(F32)
+            for o in range(nx - 1):
+                acc = acc + col_last[g, o].astype(F32)
+            wide[:, quarter(2 * g + 1)] = acc.astype(BF16).astype(F32)
+
         loop(0, ns // 2, multiply)
-        loop(1, nx, lambda o: row_copy(o).start())
+        start_group(0)
         loop(ns // 2, ns, multiply)
-        loop(1, ny, lambda o: col_copy(o).start())
-        loop(1, nx, lambda o: row_copy(o).wait_recv())
-
-        def add_row(i):
-            acc = product[i, ex, :, low].astype(F32)
-            for o in range(nx - 1):
-                acc = acc + row_in[o, i].astype(F32)
-            row_sum[i] = acc.astype(BF16)
-
-        loop(0, ny, add_row)
-        loop(1, ny, lambda o: row_pass(o).start())
-        loop(1, ny, lambda o: col_copy(o).wait_recv())
-
-        def add_col(i):
-            acc = product[ey, i, :, high].astype(F32)
-            for o in range(ny - 1):
-                acc = acc + col_in[o, i].astype(F32)
-            col_sum[i] = acc.astype(BF16)
-
-        loop(0, nx, add_col)
-        loop(1, nx, lambda o: col_pass(o).start())
-        loop(1, ny, lambda o: row_pass(o).wait_recv())
-        acc = hid_ref[:, low].astype(F32) + row_sum[ey].astype(F32)
-        for o in range(ny - 1):
-            acc = acc + row_last[o].astype(F32)
-        wide[:, low] = acc.astype(BF16).astype(F32)
-        loop(1, nx, lambda o: col_pass(o).wait_recv())
-        acc = hid_ref[:, high].astype(F32) + col_sum[ex].astype(F32)
-        for o in range(nx - 1):
-            acc = acc + col_last[o].astype(F32)
-        wide[:, high] = acc.astype(BF16).astype(F32)
+        pass_group(0)
+        start_group(1)
+        finish_group(0)
 
     sides = (low, high)
     each = pieces // 2
@@ -388,9 +403,6 @@
             target[:, at : at + 128] = flat[pl.ds(j, count, stride=each), :].astype(BF16)
 
     with jax.named_scope("route"):
-        mixed = wide[...]
-        mean = jnp.mean(mixed * mixed, axis=-1, keepdims=True)
-        normed = (mixed * lax.rsqrt(mean + EPS) * gain_ref[...]).astype(BF16)
 
         def send_rows(o, h):
             to = lax.rem(expert + o, ne)
@@ -399,22 +411,24 @@
                 {"expert": to},
             )
 
-        def placed(j):
-            return jnp.dot(place_ref[...], normed[:, j * 128 : (j + 1) * 128], preferred_element_type=F32)
-
-        for h in range(2):
+        def send_half(h):
+            scaled = (wide[:, sides[h]] * gain_ref[:, sides[h]]).astype(BF16)
+
+            def placed(j):
+                at = j * 128 - h * half
+                return jnp.dot(place_ref[...], scaled[:, at : at + 128], preferred_element_type=F32)
+
             spread(placed, packed_out, h)
             loop(1, ne, lambda o: send_rows(o, h).start())
             packed_in[h, expert] = packed_out[h, expert]
-        logits = lax.dot_general(
-            normed, router_ref[...], (((1,), (1,)), ((), ())), preferred_element_type=F32
-        )
-        scores = []
-        for k in range(pick_ref.shape[0]):
-            picked = jnp.sum(pick_ref[k] * logits, axis=-1, keepdims=True)
-            scores.append(1.0 / (1.0 + jnp.exp(-picked)))
-        all_scores = sum(scores)
-        combine_w[...] = sum((score / all_scores) * put_ref[k] for k, score in enumerate(scores))
+
+        def take_half(h):
+            loop(1, ne, lambda o: send_rows(o, h).wait_recv())
+            gather_pieces(packed_in, held.at[0], h)
+
+        send_half(0)
+        pass_group(1)
+        take_half(0)
 
     def gather_copy(stage, forward, h):
         way = 0 if forward else 1
@@ -425,25 +439,118 @@
             {"seq": right if forward else left},
         )
 
-    def return_copy(stage, forward, h):
+    def return_copy(stage, forward, u):
         way = 0 if forward else 1
         buffer = from_left if forward else from_right
         slot = 2 * (hops - stage + 1) + way_of(forward) if stage > 1 else 1
         return remote(
-            parts.at[slot, :, sides[h]], buffer.at[stage - 1, :, sides[h]],
-            r_send.at[way, h, stage - 1], r_recv.at[way, h, stage - 1], {"seq": right if forward else left},
-        )
+            parts.at[slot, :, quarter(u)], buffer.at[stage - 1, :, quarter(u)],
+            r_send.at[way, u, stage - 1], r_recv.at[way, u, stage - 1], {"seq": right if forward else left},
+        )
+
+    def q_copy(o, slot):
+        to = lax.rem(expert + o, ne)
+        return remote(
+            q_out.at[slot, to], q_in.at[slot, expert], q_send.at[slot, o - 1], q_recv.at[slot, o - 1], {"expert": to}
+        )
+
+    def t_copy(slot):
+        away = hops if slot == 1 else slot // 2 if slot % 2 else nz - slot // 2
+        to = lax.rem(plane + away, nz) * 2 + core
+        return remote(t_out.at[slot], t_in.at[slot - 1], t_send.at[slot - 1], t_recv.at[slot - 1], {"seq": to})
+
+    def k_copy(o):
+        to = lax.rem(plane + o, nz) * 2 + core
+        slot = 2 * o if o < hops else 1 if o == hops else 2 * (nz - o) + 1
+        return remote(combine_w.at[0], combine_w.at[slot], k_send.at[o - 1], k_recv.at[o - 1], {"seq": to})
+
+    def weighted(slot, h):
+        weights_all = combine_w[slot][:, :count]
+        weights_high = weights_all.astype(BF16)
+        weights_low = (weights_all - weights_high.astype(F32)).astype(BF16)
+        values = returned[:, sides[h]]
+        return jnp.dot(weights_high, values, preferred_element_type=F32) + jnp.dot(
+            weights_low, values, preferred_element_type=F32
+        )
+
+    def spread_q(slot):
+        for j in range(each):
+            at = half + j * 128
+            flat[pl.ds(j, count, stride=each), :] = parts[slot, :, at : at + 128].astype(F32)
+        q_out[slot] = flat[...].astype(BF16).reshape(q_out.shape[1:])
+        loop(1, ne, lambda o: q_copy(o, slot).start())
+        q_in[slot, expert] = q_out[slot, expert]
+
+    def take_q(slot):
+        loop(1, ne, lambda o: q_copy(o, slot).wait_recv())
+        flat[...] = q_in[slot].astype(F32).reshape(flat.shape)
+        for j in range(each):
+            at = half + j * 128
+            returned[:, at : at + 128] = flat[pl.ds(j, count, stride=each), :].astype(BF16)
+        value = weighted(slot, 1)
+        if slot == 0:
+            routed_high[...] = value
+        else:
+            t_out[slot] = value.astype(BF16)
+            t_copy(slot).start()
+
+    def spread_pair(pair):
+        spread_q(2 * pair)
+        spread_q(2 * pair + 1)
+
+    def take_pair(pair):
+        take_q(2 * pair + 1)
+        take_q(2 * pair)
 
     def way_of(forward):
         return 1 if forward else 0
 
     ways = ((True, 0, 1), (False, 1, 0))
 
+    def scale_copy(o):
+        to = lax.rem(expert + o, ne)
+        return remote(scale_out, scale_in.at[expert], c_send.at[o - 1], c_recv.at[o - 1], {"expert": to})
+
+    def plane_copy(o):
+        to = lax.rem(plane + o, nz) * 2 + core
+        slot = 2 * o if o < hops else 1 if o == hops else 2 * (nz - o) + 1
+        return remote(scale_held.at[0], scale_held.at[slot], z_send.at[o - 1], z_recv.at[o - 1], {"seq": to})
+
+    def first_row(value):
+        return jnp.where(grid((8, 128), 0) == 0, value, 0.0)
+
+    def send_scales():
+        mixed = wide[...]
+        scale = lax.rsqrt(jnp.mean(mixed * mixed, axis=-1, keepdims=True) + EPS)
+        scale_out[...] = first_row(jnp.sum(scale * (put_ref[0] + put_ref[1]), axis=0, keepdims=True))
+        loop(1, ne, lambda o: scale_copy(o).start())
+        scale_in[expert] = scale_out[...]
+        return (mixed * scale * gain_ref[...]).astype(BF16)
+
+    def take_scales():
+        loop(1, ne, lambda o: scale_copy(o).wait_recv())
+        rows_in = jnp.sum(scale_in[...], axis=1)
+        row, source = grid((count, ne), 0), grid((count, ne), 1)
+        sender = ((row >= source * cap) & (row < (source + 1) * cap)).astype(F32)
+        spread_rows = jnp.dot(sender, rows_in, preferred_element_type=F32, precision=lax.Precision.HIGHEST)
+        passed = jnp.sum((row >= (source + 1) * cap).astype(F32), axis=1, keepdims=True)
+        lane, place = grid((count, 128), 1).astype(F32), grid((count, 128), 0).astype(F32)
+        wanted = (expert * cap).astype(F32) + place - cap * passed
+        column = jnp.sum(jnp.where(lane == wanted, spread_rows, 0.0), axis=1, keepdims=True)
+        scale_held[0] = first_row(jnp.sum(jnp.where(lane == place, column, 0.0), axis=0, keepdims=True))
+        for o in range(1, nz):
+            plane_copy(o).start()
+
+    def scale_column(slot):
+        lane, place = grid((count, 128), 1), grid((count, 128), 0)
+        return jnp.sum(jnp.where(lane == place, scale_held[slot, 0:1, :], 0.0), axis=1, keepdims=True)
+
     def compute(pair):
         rows = held[2 * pair : 2 * pair + 2].reshape(2 * count, width)
+        scale = jnp.concatenate([scale_column(2 * pair), scale_column(2 * pair + 1)], axis=0)
         across = (((1,), (1,)), ((), ()))
-        gate = lax.dot_general(rows, gate_w[...], across, preferred_element_type=F32)
-        up = lax.dot_general(rows, up_w[...], across, preferred_element_type=F32)
+        gate = lax.dot_general(rows, gate_w[...], across, preferred_element_type=F32) * scale
+        up = lax.dot_general(rows, up_w[...], across, preferred_element_type=F32) * scale
         hidden[...] = (gate / (1.0 + jnp.exp(-gate)) * up).astype(BF16)
         step = min(width, 512)
 
@@ -454,36 +561,67 @@
 
         loop(0, width // step, down)
 
+    def start_gather(stage, h):
+        for forward, early, late in ways:
+            if stage < hops or h == early:
+                gather_copy(stage, forward, h).start()
+
+    def wait_gather(stage, h):
+        for forward, early, late in ways:
+            gather_copy(stage, forward, h).wait_recv()
+
     with jax.named_scope("experts"):
-        for h in range(2):
-            loop(1, ne, lambda o: send_rows(o, h).wait_recv())
-            gather_pieces(packed_in, held.at[0], h)
-            for forward, early, late in ways:
-                if hops > 1 or h == early:
-                    gather_copy(1, forward, h).start()
+        start_gather(1, 0)
+        finish_group(1)
+        send_half(1)
+        normed = send_scales()
+        if hops > 2:
+            wait_gather(1, 0)
+            start_gather(2, 0)
+        take_half(1)
+        start_gather(1, 1)
+        take_scales()
+        logits = lax.dot_general(
+            normed, router_ref[...], (((1,), (1,)), ((), ())), preferred_element_type=F32
+        )
+        scores = []
+        for k in range(pick_ref.shape[0]):
+            picked = jnp.sum(pick_ref[k] * logits, axis=-1, keepdims=True)
+            scores.append(1.0 / (1.0 + jnp.exp(-picked)))
+        all_scores = sum(scores)
+        combine_w[0] = sum((score / all_scores) * put_ref[k] for k, score in enumerate(scores))
+        for o in range(1, nz):
+            k_copy(o).start()
         for copy in loads:
             copy.wait()
         for copy in pairs:
             copy.wait_recv()
-        for stage in range(1, hops - 1):
-            last = stage == hops - 2
-            for h in range(2):
-                for forward, early, late in ways:
-                    gather_copy(stage, forward, h).wait_recv()
-                    if not last or h == early:
-                        gather_copy(stage + 1, forward, h).start()
-            compute(stage)
+        for o in range(1, nz):
+            plane_copy(o).wait_recv()
+        if hops > 2:
+            wait_gather(1, 1)
+            start_gather(2, 1)
+            wait_gather(2, 0)
+            gather_copy(3, True, 0).start()
+            compute(1)
+            wait_gather(2, 1)
+            gather_copy(3, False, 1).start()
+            spread_pair(1)
+            compute(2)
         for forward, early, late in ways:
             if hops > 1:
                 gather_copy(hops - 1, forward, early).wait_recv()
                 gather_copy(hops, forward, early).start()
                 if hops > 2:
                     gather_copy(hops - 1, forward, late).start()
+        if hops > 2:
+            spread_pair(2)
         for forward, early, late in ways:
             gather_copy(hops, forward, early).wait_recv()
         compute(0)
         for forward, early, late in ways:
             return_copy(1, forward, early).start()
+        spread_pair(0)
         if hops > 1:
             for forward, early, late in ways:
                 gather_copy(hops - 1, forward, late).wait_recv()
@@ -491,16 +629,25 @@
 
     with jax.named_scope("combine"):
         for stage in range(2, hops + 1):
-            for h in range(2):
+            for u in range(2):
                 for forward, early, late in ways:
-                    if stage > 2 or h == early:
-                        return_copy(stage - 1, forward, h).wait_recv()
+                    if stage > 2 or u == early:
+                        return_copy(stage - 1, forward, u).wait_recv()
                         buffer = from_left if forward else from_right
                         slot = 2 * (hops - stage + 1) + way_of(forward)
-                        parts[slot, :, sides[h]] = (
-                            parts[slot, :, sides[h]].astype(F32) + buffer[stage - 2, :, sides[h]].astype(F32)
+                        parts[slot, :, quarter(u)] = (
+                            parts[slot, :, quarter(u)].astype(F32) + buffer[stage - 2, :, quarter(u)].astype(F32)
                         ).astype(BF16)
-                    return_copy(stage, forward, h).start()
+                    return_copy(stage, forward, u).start()
+            if stage == 2:
+                spread_pair(hops - 1)
+                for o in range(1, nz):
+                    k_copy(o).wait_recv()
+            take_pair(stage - 1)
+        if hops == 1:
+            for o in range(1, nz):
+                k_copy(o).wait_recv()
+        take_pair(0)
 
     with jax.named_scope("home"):
 
@@ -508,7 +655,7 @@
             at = pl.ds(j * 128, 128)
             value = parts[0, :, at].astype(F32)
             for forward, early, late in ways:
-                if hops > 1 or j // each == early:
+                if hops > 1 or 2 * j // each == early:
                     buffer = from_left if forward else from_right
                     value = value + buffer[hops - 1, :, at].astype(F32)
             return value
@@ -520,24 +667,25 @@
                 {"expert": to},
             )
 
-        for h in range(2):
-            for forward, early, late in ways:
-                if hops > 1 or h == early:
-                    return_copy(hops, forward, h).wait_recv()
-            spread(summed_piece, back_out, h)
-            loop(1, ne, lambda o: send_back(o, h).start())
-            back_in[h, expert] = back_out[h, expert]
-        weights_high = combine_w[...].astype(BF16)
-        weights_low = (combine_w[...] - weights_high.astype(F32)).astype(BF16)
-        for h in range(2):
-            loop(1, ne, lambda o: send_back(o, h).wait_recv())
-            gather_pieces(back_in, returned, h)
-            values = returned[:, sides[h]]
-            routed = jnp.dot(weights_high, values, preferred_element_type=F32) + jnp.dot(
-                weights_low, values, preferred_element_type=F32
-            )
+        def finish_half(h, routed):
             mixed = (wide[:, sides[h]] + routed).astype(BF16)
             out_ref[:, :, sides[h]] = mixed.reshape(out_ref.shape[:2] + (half,))
+
+        for u in range(2):
+            for forward, early, late in ways:
+                if hops > 1 or u == early:
+                    return_copy(hops, forward, u).wait_recv()
+        spread(summed_piece, back_out, 0)
+        loop(1, ne, lambda o: send_back(o, 0).start())
+        back_in[0, expert] = back_out[0, expert]
+        total = routed_high[...]
+        for slot in range(1, nz):
+            t_copy(slot).wait_recv()
+            total = total + t_in[slot - 1].astype(F32)
+        finish_half(1, total)
+        loop(1, ne, lambda o: send_back(o, 0).wait_recv())
+        gather_pieces(back_in, returned, 0)
+        finish_half(0, weighted(0, 0))
 
     with jax.named_scope("finish"):
 
@@ -546,20 +694,29 @@
             proj_copy(o).wait_send()
             for h in range(2):
                 send_rows(o, h).wait_send()
-                send_back(o, h).wait_send()
+            send_back(o, 0).wait_send()
+            for slot in range(nz):
+                q_copy(o, slot).wait_send()
 
         loop(1, ne, sent_peers)
 
-        def sent_rows(o):
-            row_copy(o).wait_send()
-            col_pass(o).wait_send()
-
-        def sent_cols(o):
-            col_copy(o).wait_send()
-            row_pass(o).wait_send()
-
-        loop(1, nx, sent_rows)
-        loop(1, ny, sent_cols)
+        loop(1, ne, lambda o: scale_copy(o).wait_send())
+        for o in range(1, nz):
+            plane_copy(o).wait_send()
+            k_copy(o).wait_send()
+            t_copy(o).wait_send()
+        for g in range(2):
+
+            def sent_rows(o):
+                row_copy(o, g).wait_send()
+                col_pass(o, g).wait_send()
+
+            def sent_cols(o):
+                col_copy(o, g).wait_send()
+                row_pass(o, g).wait_send()
+
+            loop(1, nx, sent_rows)
+            loop(1, ny, sent_cols)
         loop(plane + 1, nz, lambda to: state_copy(to, plane).wait_send())
         half_copy.wait_send()
         enter_copy.wait_send()
@@ -607,7 +764,7 @@
             vmem((own, width), BF16),
             vmem((count, own), BF16),
             vmem((picks, own, ne), F32),
-            vmem((picks, own, count), F32),
+            vmem((picks, own, 128), F32),
             vmem((ne, own, lanes), BF16),
             vmem((ne - 1, own, lanes), BF16),
             vmem((own, lanes), BF16),
@@ -624,24 +781,32 @@
             vmem((tokens, channels), BF16),
             vmem((ns,) + w.shape, BF16),
             vmem((ny, nx, own, width), BF16),
-            vmem((nx - 1, ny, own, half), BF16),
-            vmem((ny, own, half), BF16),
-            vmem((ny - 1, own, half), BF16),
-            vmem((ny - 1, nx, own, half), BF16),
-            vmem((nx, own, half), BF16),
-            vmem((nx - 1, own, half), BF16),
+            vmem((2, nx - 1, ny, own, half // 2), BF16),
+            vmem((2, ny, own, half // 2), BF16),
+            vmem((2, ny - 1, own, half // 2), BF16),
+            vmem((2, ny - 1, nx, own, half // 2), BF16),
+            vmem((2, nx, own, half // 2), BF16),
+            vmem((2, nx - 1, own, half // 2), BF16),
+            vmem((8, 128), F32),
+            vmem((ne, 8, 128), F32),
+            vmem((nz, 8, 128), F32),
             vmem((own, width), F32),
-            vmem((own, count), F32),
+            vmem((nz, own, 128), F32),
             vmem((count * pieces // 2, 128), F32),
             vmem((2, ne, cap * pieces // 2, 128), BF16),
             vmem((2, ne, cap * pieces // 2, 128), BF16),
-            vmem((2, ne, cap * pieces // 2, 128), BF16),
-            vmem((2, ne, cap * pieces // 2, 128), BF16),
+            vmem((1, ne, cap * pieces // 2, 128), BF16),
+            vmem((1, ne, cap * pieces // 2, 128), BF16),
             vmem((count, width), BF16),
+            vmem((nz, ne, cap * pieces // 2, 128), BF16),
+            vmem((nz, ne, cap * pieces // 2, 128), BF16),
+            vmem((nz, own, half), BF16),
+            vmem((nz - 1, own, half), BF16),
+            vmem((own, half), F32),
             vmem((nz, count, width), BF16),
             vmem((nz, count, width), BF16),
-            vmem((hops, count, width), BF16),
-            vmem((hops, count, width), BF16),
+            vmem((hops, count, half), BF16),
+            vmem((hops, count, half), BF16),
             vmem((2 * units, width), BF16),
             vmem((2 * units, width), BF16),
             vmem((2 * units, width), BF16),
@@ -654,12 +819,17 @@
             dma((nz,)), dma((nz,)),
             dma((2, hops)), dma((2, hops)),
             dma((nz,)), dma((nz,)),
-            dma((2, nx + ny)), dma((2, nx + ny)),
-            dma((2, nx + ny)), dma((2, nx + ny)),
+            dma((4, nx + ny)), dma((4, nx + ny)),
+            dma((4, nx + ny)), dma((4, nx + ny)),
+            dma((ne - 1,)), dma((ne - 1,)),
+            dma((nz - 1,)), dma((nz - 1,)),
             dma((2, ne - 1)), dma((2, ne - 1)),
             dma((2, ne - 1)), dma((2, ne - 1)),
             dma((2, 2, hops)), dma((2, 2, hops)),
             dma((2, 2, hops)), dma((2, 2, hops)),
+            dma((nz, ne - 1)), dma((nz, ne - 1)),
+            dma((nz - 1,)), dma((nz - 1,)),
+            dma((nz - 1,)), dma((nz - 1,)),
         ],
         compiler_params=pltpu.CompilerParams(
             collective_id=0, has_side_effects=True, vmem_limit_bytes=58 * 1024 * 1024

time: 187 us -> 175 us (0.936)
  Pallas kernels: 185 us -> 174 us
    pallas_call x1, Pallas kernels: 185 us -> 174 us  [layer_call(): pl.pallas_call(functools.partial(layer_kernel, ns, ne, cap), out_shape=ja...]
where the time goes in v4:
time: 175 us
  Pallas kernels  174 us (99%)
    pallas_call x1, Pallas kernels, layer_call(): pl.pallas_call(functools.partial(layer_kernel, ns, ne, cap), out_shape=ja...  174 us

profile of v4, /device:TPU:2, one launch (start us, length us, event | category | flops | bytes accessed | tf_op | source)
XLA Modules:
  0.0 175.2 jit_solution(9035775261916606410)
XLA Ops:
  0.0 173.5 %shard_map.145 = bf16[8,2,4096]{2,1,0:T(2,128)(2,1)} custom-call(bf16[128,2,256]{2,1,0:T(2,128)(2,1)} %x_in.1, bf16[128,2,256]{2,1,0:T(2,128)(2,1)} %z_in.1, bf16[288,256]{1,0:T(8,128)(2,1)} %bitcast.19, bf16[256,256]{1,0:T(8,128)(2,1)} %dtw_ref.1, f32[1,256]{1,0:T(1,128)} %bitcast.24, f32[16,256]{1,0:T(8,128)} %bitcast.21, f32[1,256]{1,0:T(1,128)} %bitcast.25, ...), custom_call_target="tpu_custom_call" | custom-call | tf_op jit(solution)/shard_map/pallas_call | solution.py:756
  173.5 1.7 copy.17

commit v5 on v4

--- a/solution.py
+++ b/solution.py
@@ -57,7 +57,7 @@
     product, row_in, row_sum, row_last, col_in, col_sum, col_last,
     scale_out, scale_in, scale_held,
     wide, combine_w, flat, packed_out, packed_in, back_out, back_in, returned,
-    q_out, q_in, t_out, t_in, routed_high,
+    q_out, q_in, t_out, t_left, t_right, routed_high,
     held, parts, from_left, from_right, gate_w, up_w, down_w, hidden,
     load_sem, pair_send, pair_recv, p1_send, p1_recv, p2_send, p2_recv,
     h_send, h_recv, s_send, s_recv, ring_send, ring_recv, sib_send, sib_recv,
@@ -454,10 +454,15 @@
             q_out.at[slot, to], q_in.at[slot, expert], q_send.at[slot, o - 1], q_recv.at[slot, o - 1], {"expert": to}
         )
 
-    def t_copy(slot):
-        away = hops if slot == 1 else slot // 2 if slot % 2 else nz - slot // 2
-        to = lax.rem(plane + away, nz) * 2 + core
-        return remote(t_out.at[slot], t_in.at[slot - 1], t_send.at[slot - 1], t_recv.at[slot - 1], {"seq": to})
+    def t_copy(stage, forward, u):
+        way = 0 if forward else 1
+        buffer = t_left if forward else t_right
+        slot = 2 * (hops - stage + 1) + way_of(forward) if stage > 1 else 1
+        picked = quarter(u) if stage == 1 else pl.ds(0, half)
+        return remote(
+            t_out.at[slot, :, picked], buffer.at[stage - 1, :, picked],
+            t_send.at[way, stage - 1], t_recv.at[way, stage - 1], {"seq": right if forward else left},
+        )
 
     def k_copy(o):
         to = lax.rem(plane + o, nz) * 2 + core
@@ -492,7 +497,6 @@
             routed_high[...] = value
         else:
             t_out[slot] = value.astype(BF16)
-            t_copy(slot).start()
 
     def spread_pair(pair):
         spread_q(2 * pair)
@@ -501,6 +505,57 @@
     def take_pair(pair):
         take_q(2 * pair + 1)
         take_q(2 * pair)
+
+    def t_stage(stage):
+        for forward, early, late in ways:
+            if stage > 1:
+                t_copy(stage - 1, forward, early).wait_recv()
+                buffer = t_left if forward else t_right
+                slot = 2 * (hops - stage + 1) + way_of(forward)
+                picked = quarter(early) if stage == 2 else pl.ds(0, half)
+                t_out[slot, :, picked] = (
+                    t_out[slot, :, picked].astype(F32) + buffer[stage - 2, :, picked].astype(F32)
+                ).astype(BF16)
+            t_copy(stage, forward, early).start()
+
+    def sent_early():
+        def sent_peers(o):
+            part_copy(o).wait_send()
+            proj_copy(o).wait_send()
+            scale_copy(o).wait_send()
+            for h in range(2):
+                send_rows(o, h).wait_send()
+
+        loop(1, ne, sent_peers)
+        for g in range(2):
+
+            def sent_rows(o):
+                row_copy(o, g).wait_send()
+                col_pass(o, g).wait_send()
+
+            def sent_cols(o):
+                col_copy(o, g).wait_send()
+                row_pass(o, g).wait_send()
+
+            loop(1, nx, sent_rows)
+            loop(1, ny, sent_cols)
+        loop(plane + 1, nz, lambda to: state_copy(to, plane).wait_send())
+        half_copy.wait_send()
+        enter_copy.wait_send()
+        for stage in range(1, hops + 1):
+            ring_copy(stage, True).wait_send()
+        for stage in range(1, back + 1):
+            ring_copy(stage, False).wait_send()
+        loop(0, nz, lambda i: sibling_copy(2 * i + core).wait_send())
+        for copy in pairs:
+            copy.wait_send()
+
+    def sent_pair(pair):
+        def sent(o):
+            q_copy(o, 2 * pair).wait_send()
+            q_copy(o, 2 * pair + 1).wait_send()
+
+        loop(1, ne, sent)
 
     def way_of(forward):
         return 1 if forward else 0
@@ -552,14 +607,18 @@
         gate = lax.dot_general(rows, gate_w[...], across, preferred_element_type=F32) * scale
         up = lax.dot_general(rows, up_w[...], across, preferred_element_type=F32) * scale
         hidden[...] = (gate / (1.0 + jnp.exp(-gate)) * up).astype(BF16)
-        step = min(width, 512)
+        finish_compute(pair, 0)
+
+    def finish_compute(pair, h):
+        step = min(half, 512)
+        blocks_half = half // step
 
         def down(b):
             at = pl.multiple_of(b * step, step)
             out = jnp.dot(hidden[...], down_w[:, pl.ds(at, step)], preferred_element_type=F32)
             parts[2 * pair : 2 * pair + 2, :, pl.ds(at, step)] = out.astype(BF16).reshape(2, count, step)
 
-        loop(0, width // step, down)
+        loop(h * blocks_half, (h + 1) * blocks_half, down)
 
     def start_gather(stage, h):
         for forward, early, late in ways:
@@ -598,16 +657,19 @@
             copy.wait_recv()
         for o in range(1, nz):
             plane_copy(o).wait_recv()
+        sent_early()
         if hops > 2:
             wait_gather(1, 1)
             start_gather(2, 1)
             wait_gather(2, 0)
             gather_copy(3, True, 0).start()
             compute(1)
+            finish_compute(1, 1)
             wait_gather(2, 1)
             gather_copy(3, False, 1).start()
             spread_pair(1)
             compute(2)
+            finish_compute(2, 1)
         for forward, early, late in ways:
             if hops > 1:
                 gather_copy(hops - 1, forward, early).wait_recv()
@@ -621,7 +683,7 @@
         compute(0)
         for forward, early, late in ways:
             return_copy(1, forward, early).start()
-        spread_pair(0)
+        finish_compute(0, 1)
         if hops > 1:
             for forward, early, late in ways:
                 gather_copy(hops - 1, forward, late).wait_recv()
@@ -640,14 +702,37 @@
                         ).astype(BF16)
                     return_copy(stage, forward, u).start()
             if stage == 2:
+                finish_compute(hops - 1, 1)
+                spread_pair(0)
                 spread_pair(hops - 1)
                 for o in range(1, nz):
                     k_copy(o).wait_recv()
-            take_pair(stage - 1)
+            elif stage == 3:
+                take_pair(0)
+                t_stage(1)
+                sent_pair(1)
+                sent_pair(2)
         if hops == 1:
+            spread_pair(0)
             for o in range(1, nz):
                 k_copy(o).wait_recv()
-        take_pair(0)
+        if hops < 3:
+            take_pair(0)
+            t_stage(1)
+        for stage in range(2, hops + 1):
+            take_pair(hops - stage + 1)
+            t_stage(stage)
+        sent_pair(0)
+        if hops > 1:
+            sent_pair(hops - 1)
+        for stage in range(1, hops + 1):
+            for forward, early, late in ways:
+                for h in range(2):
+                    if stage < hops or h == early:
+                        gather_copy(stage, forward, h).wait_send()
+        for o in range(1, nz):
+            plane_copy(o).wait_send()
+            k_copy(o).wait_send()
 
     with jax.named_scope("home"):
 
@@ -678,61 +763,25 @@
         spread(summed_piece, back_out, 0)
         loop(1, ne, lambda o: send_back(o, 0).start())
         back_in[0, expert] = back_out[0, expert]
-        total = routed_high[...]
-        for slot in range(1, nz):
-            t_copy(slot).wait_recv()
-            total = total + t_in[slot - 1].astype(F32)
-        finish_half(1, total)
+        for forward, early, late in ways:
+            t_copy(hops, forward, early).wait_recv()
+            buffer = t_left if forward else t_right
+            picked = quarter(early) if hops == 1 else pl.ds(0, half)
+            routed_high[:, picked] += buffer[hops - 1, :, picked].astype(F32)
+        finish_half(1, routed_high[...])
         loop(1, ne, lambda o: send_back(o, 0).wait_recv())
         gather_pieces(back_in, returned, 0)
         finish_half(0, weighted(0, 0))
 
     with jax.named_scope("finish"):
 
-        def sent_peers(o):
-            part_copy(o).wait_send()
-            proj_copy(o).wait_send()
-            for h in range(2):
-                send_rows(o, h).wait_send()
-            send_back(o, 0).wait_send()
-            for slot in range(nz):
-                q_copy(o, slot).wait_send()
-
-        loop(1, ne, sent_peers)
-
-        loop(1, ne, lambda o: scale_copy(o).wait_send())
-        for o in range(1, nz):
-            plane_copy(o).wait_send()
-            k_copy(o).wait_send()
-            t_copy(o).wait_send()
-        for g in range(2):
-
-            def sent_rows(o):
-                row_copy(o, g).wait_send()
-                col_pass(o, g).wait_send()
-
-            def sent_cols(o):
-                col_copy(o, g).wait_send()
-                row_pass(o, g).wait_send()
-
-            loop(1, nx, sent_rows)
-            loop(1, ny, sent_cols)
-        loop(plane + 1, nz, lambda to: state_copy(to, plane).wait_send())
-        half_copy.wait_send()
-        enter_copy.wait_send()
+        loop(1, ne, lambda o: send_back(o, 0).wait_send())
         for stage in range(1, hops + 1):
-            ring_copy(stage, True).wait_send()
             for forward, early, late in ways:
+                t_copy(stage, forward, early).wait_send()
                 for h in range(2):
-                    if stage < hops or h == early:
-                        gather_copy(stage, forward, h).wait_send()
                     if stage > 1 or h == early:
                         return_copy(stage, forward, h).wait_send()
-        for stage in range(1, back + 1):
-            ring_copy(stage, False).wait_send()
-        loop(0, nz, lambda i: sibling_copy(2 * i + core).wait_send())
-        for copy in pairs:
-            copy.wait_send()
 
 
 def layer_call(
@@ -801,7 +850,8 @@
             vmem((nz, ne, cap * pieces // 2, 128), BF16),
             vmem((nz, ne, cap * pieces // 2, 128), BF16),
             vmem((nz, own, half), BF16),
-            vmem((nz - 1, own, half), BF16),
+            vmem((hops, own, half), BF16),
+            vmem((hops, own, half), BF16),
             vmem((own, half), F32),
             vmem((nz, count, width), BF16),
             vmem((nz, count, width), BF16),
@@ -828,7 +878,7 @@
             dma((2, 2, hops)), dma((2, 2, hops)),
             dma((2, 2, hops)), dma((2, 2, hops)),
             dma((nz, ne - 1)), dma((nz, ne - 1)),
-            dma((nz - 1,)), dma((nz - 1,)),
+            dma((2, hops)), dma((2, hops)),
             dma((nz - 1,)), dma((nz - 1,)),
         ],
         compiler_params=pltpu.CompilerParams(

time: 175 us -> 172 us (0.983)
  Pallas kernels: 174 us -> 170 us
    pallas_call x1, Pallas kernels: 174 us -> 170 us  [layer_call(): pl.pallas_call(functools.partial(layer_kernel, ns, ne, cap), out_shape=ja...]
where the time goes in v5:
time: 172 us; the launch traced here: 171 us
  Pallas kernels  170 us (99%)
    pallas_call x1, Pallas kernels, layer_call(): pl.pallas_call(functools.partial(layer_kernel, ns, ne, cap), out_shape=ja...  170 us

profile of v5, /device:TPU:2, one launch (start us, length us, event | category | flops | bytes accessed | tf_op | source)
XLA Modules:
  0.0 171.3 jit_solution(17569016369313300756)
XLA Ops:
  0.0 169.6 %shard_map.145 = bf16[8,2,4096]{2,1,0:T(2,128)(2,1)} custom-call(bf16[128,2,256]{2,1,0:T(2,128)(2,1)} %x_in.1, bf16[128,2,256]{2,1,0:T(2,128)(2,1)} %z_in.1, bf16[288,256]{1,0:T(8,128)(2,1)} %bitcast.19, bf16[256,256]{1,0:T(8,128)(2,1)} %dtw_ref.1, f32[1,256]{1,0:T(1,128)} %bitcast.24, f32[16,256]{1,0:T(8,128)} %bitcast.21, f32[1,256]{1,0:T(1,128)} %bitcast.25, ...), custom_call_target="tpu_custom_call" | custom-call | tf_op jit(solution)/shard_map/pallas_call | solution.py:805
  169.6 1.7 copy.17

commit v6 on v5

--- a/solution.py
+++ b/solution.py
@@ -667,7 +667,6 @@
             finish_compute(1, 1)
             wait_gather(2, 1)
             gather_copy(3, False, 1).start()
-            spread_pair(1)
             compute(2)
             finish_compute(2, 1)
         for forward, early, late in ways:
@@ -677,6 +676,7 @@
                 if hops > 2:
                     gather_copy(hops - 1, forward, late).start()
         if hops > 2:
+            spread_pair(1)
             spread_pair(2)
         for forward, early, late in ways:
             gather_copy(hops, forward, early).wait_recv()

time: 172 us -> 172 us (level)
  no operation moved by 1% of the time
where the time goes in v6:
time: 172 us; the launch traced here: 170 us
  Pallas kernels  169 us (98%)
    pallas_call x1, Pallas kernels, layer_call(): pl.pallas_call(functools.partial(layer_kernel, ns, ne, cap), out_shape=ja...  169 us

profile of v6, /device:TPU:2, one launch (start us, length us, event | category | flops | bytes accessed | tf_op | source)
XLA Modules:
  0.0 170.5 jit_solution(17230109894080503924)
XLA Ops:
  0.0 168.8 %shard_map.145 = bf16[8,2,4096]{2,1,0:T(2,128)(2,1)} custom-call(bf16[128,2,256]{2,1,0:T(2,128)(2,1)} %x_in.1, bf16[128,2,256]{2,1,0:T(2,128)(2,1)} %z_in.1, bf16[288,256]{1,0:T(8,128)(2,1)} %bitcast.19, bf16[256,256]{1,0:T(8,128)(2,1)} %dtw_ref.1, f32[1,256]{1,0:T(1,128)} %bitcast.24, f32[16,256]{1,0:T(8,128)} %bitcast.21, f32[1,256]{1,0:T(1,128)} %bitcast.25, ...), custom_call_target="tpu_custom_call" | custom-call | tf_op jit(solution)/shard_map/pallas_call | solution.py:805
  168.8 1.7 copy.17
